TPU v7x, 32 devices: a whole 2x2x4 slice. The times are simulated.
32 devices in a mesh: row: 4 (over y, x), col: 8 (over z, core).
Axes of the slice: x: 2, y: 2, z: 4, core: 2. Of those that a mesh axis runs over, the one named last changes fastest.
Arguments:
- adjoint: bfloat16 [64, 16384], P(None, ('row', 'col')), may hold values from -6 to 6
- panel_order: int32 [4, 4096], P('row'), may hold values from 0 to 4095, each once within a row
- left_factor: bfloat16 [64, 64, 16, 256], P('row', 'col'), may hold values from -0.375 to 0.375
- right_factor: bfloat16 [64, 64, 16, 256], P('row', 'col'), may hold values from -0.1875 to 0.1875
- tile_ranks: int32 [64, 64], P('row', 'col'), may hold values from 1 to 16
- near_blocks: bfloat16 [4, 8, 8, 256, 256], P('row', 'col'), may hold values from -0.1875 to 0.1875
- near_index: int32 [4, 8, 2, 8], P('row', 'col'), may hold values from 0 to 15, as said below
- near_count: int32 [4, 8], P('row', 'col'), may hold values from 1 to 8, as said below
Outputs:
- result: float32 [64, 16384], P(None, ('col', 'row'))
Inputs may be any that keep to these rules, and one draw needn't show every extreme that they name: `near_index`: the 8 slots of one device name distinct tiles of its 16 x 8 block. `near_count`: some device uses all 8 slots.
All inputs are finite; a program needn't handle non-finite values.
Results may differ from a plain program's by a relative error of at most 0.0017.
Values may be sent and summed in bfloat16 or wider, within the bound.
No kernel may reach another device: no remote copies, remote signals or barrier semaphores. Data moves between devices by JAX's collectives and lax.ppermute only.
A program may use at most 64 MiB of HBM per device.

v0:
```python
import jax
import jax.numpy as jnp
from jax import lax
from jax.sharding import PartitionSpec as P


def local(
    adjoint, panel_order, left_factor, right_factor, tile_ranks, near_blocks, near_index, near_count
):
    width_cols = adjoint.shape[0]
    row_count, col_count, rank_most, tile_width = left_factor.shape
    slot_most = near_blocks.shape[2]
    gathered = lax.all_gather(adjoint, "col", axis=1, tiled=True)
    tiled = jnp.take(gathered, panel_order[0], axis=1).reshape(width_cols, row_count, tile_width)
    blocks = near_blocks[0, 0]
    row_list = near_index[0, 0, 0]
    col_list = near_index[0, 0, 1]
    used_slots = near_count[0, 0]
    picked = tiled[:, row_list, :]
    product = jnp.einsum("knb,nbc->knc", picked, blocks, preferred_element_type=jnp.float32)
    valid = jnp.arange(slot_most, dtype=jnp.int32) < used_slots
    product = jnp.where(valid[None, :, None], product, 0.0)
    onehot = (col_list[:, None] == jnp.arange(col_count, dtype=jnp.int32)[None, :]).astype(
        jnp.float32
    )
    near_part = jnp.einsum("knc,nt->ktc", product, onehot, precision=lax.Precision.HIGHEST)
    projected = jnp.einsum("kab,acrb->ackr", tiled, left_factor, preferred_element_type=jnp.float32)
    keep = (jnp.arange(rank_most, dtype=jnp.int32)[None, None, :] < tile_ranks[:, :, None])[
        :, :, None, :
    ]
    projected = jnp.where(keep, projected, 0.0).astype(jnp.bfloat16)
    far_part = jnp.einsum(
        "ackr,acrb->kcb", projected, right_factor, preferred_element_type=jnp.float32
    )
    partial_value = (far_part + near_part).reshape(width_cols, col_count * tile_width)
    return lax.psum_scatter(partial_value, "row", scatter_dimension=1, tiled=True)


def solution(mesh):
    placed = (
        P(None, ("row", "col")),
        P("row", None),
        P("row", "col", None, None),
        P("row", "col", None, None),
        P("row", "col"),
        P("row", "col", None, None, None),
        P("row", "col", None, None),
        P("row", "col"),
    )
    return jax.shard_map(
        local, mesh=mesh, in_specs=placed, out_specs=P(None, ("col", "row")), check_vma=False
    )
```

profile of v0, /device:TPU:0, one launch (start us, length us, event | category | flops | bytes accessed | tf_op | source)
XLA Modules:
  0.0 79.7 jit_solution(256525380908972910)
XLA Ops:
  6.5 0.0 copy-start
  6.5 0.0 copy-start.3
  6.5 0.0 reduce-scatter.2.cloned.1.call-start
  6.5 0.8 fusion.23
  7.3 0.0 copy-done.3
  7.3 1.0 %copy.12 = bf16[64,512]{0,1:T(8,128)(2,1)S(1)} copy(bf16[64,512]{1,0:T(8,128)(2,1)} %param.8) | data formatting | bytes 131072 | tf_op args[0]
  8.3 0.0 copy-start.1
  8.3 18.4 %all_gather.3 = bf16[64,4096]{0,1:T(8,128)(2,1)S(1)} all-gather(bf16[64,512]{0,1:T(8,128)(2,1)S(1)} %copy.12), channel_id=1, replica_groups=mesh['row'=4,'col'=8] {'col'}, dimensions={1}, use_global_device_ids=true | all-gather | bytes 589824 | tf_op jit(solution)/shard_map/all_gather | solution.py:13
  26.7 0.0 copy-done.1
  26.7 0.5 broadcast.82
  27.2 0.7 reduce.3
  27.9 0.0 copy-start.2
  28.6 0.0 copy-done.2
  28.6 0.1 iota_compare_fusion
  28.7 12.1 %gather_fusion = bf16[4096,64]{1,0:T(8,128)(2,1)S(1)} fusion(bf16[64,4096]{0,1:T(8,128)(2,1)S(1)} %all_gather.3, s32[4096]{0:T(1024)S(1)} %broadcast_clamp_fusion), kind=kCustom, calls=%fused_computation | custom fusion | bytes 1064960 | tf_op jit(solution)/shard_map/jit(_take)/gather | solution.py:14
  40.9 0.7 broadcast_select_fusion
  41.6 0.6 gather_fusion.1
  42.3 0.0 copy-done
  42.3 0.3 fusion.6
  42.6 0.7 fusion.13
  43.3 2.3 %fusion.5 = f32[8,8,8,256]{3,2,1,0:T(8,128)S(1)} fusion(bf16[64,16,256]{0,2,1:T(8,128)(2,1)S(1)} %broadcast_select_fusion, bf16[16,8,16,256]{3,2,1,0:T(8,128)(2,1)} %param.10, bf16[16,8,16,256]{3,2,1,0:T(8,128)(2,1)} %param.11, f32[8,64,256]{2,0,1:T(8,128)S(1)} %fusion.13, pred[16,8,16]{2,0,1:T(8,128)(4,1)S(1)} %iota_compare_fusion), kind=kOutput, calls=%fused_computation.8 | convolution fusion | flops 134610944 | bytes 3672064 | tf_op jit(solution)/shard_map/ackr,acrb->kcb/dot_general | solution.py:32
  45.6 0.8 %copy.19 = f32[8,8,8,256]{3,2,0,1:T(8,128)} copy(f32[8,8,8,256]{3,2,1,0:T(8,128)S(1)} %fusion.5) | data formatting | bytes 1048576 | tf_op jit(solution)/shard_map/reshape | solution.py:35
  46.4 0.0 reduce-scatter.2.cloned.1.call-update
  46.4 26.4 %reduce-scatter.2.cloned.1.call-done = f32[64,512]{1,0:T(8,128)} async-done(((f32[64,2048]{1,0:T(8,128)}), f32[64,512]{1,0:T(8,128)}) %reduce-scatter.2.cloned.1.call-update) | async-done | bytes 131088 | tf_op jit(solution)/shard_map/reduce_scatter | solution.py:36
  (7 shorter events, 0.1 us)
Async XLA Ops:
  6.5 35.7 %copy-start = (bf16[1,1,8,256,256]{4,3,2,1,0:T(8,128)(2,1)S(1)}, bf16[1,1,8,256,256]{4,3,2,1,0:T(8,128)(2,1)}, u32[]{:S(2)}) copy-start(bf16[1,1,8,256,256]{4,3,2,1,0:T(8,128)(2,1)} %param.13) | copy-start | bytes 3145732
  6.5 0.8 copy-start.3
  6.5 66.3 %reduce-scatter.2.cloned.1.call-start = ((), (), s32[]{:S(2)}) async-start(), calls=%async_computation.1 | async-start | bytes 655360 | tf_op jit(solution)/shard_map/reduce_scatter | solution.py:36
  8.3 18.4 %copy-start.1 = (s32[1,4096]{1,0:T(1,128)S(1)}, s32[1,4096]{1,0:T(1,128)}, u32[]{:S(2)}) copy-start(s32[1,4096]{1,0:T(1,128)} %param.9) | copy-start | bytes 49156
  27.9 0.7 copy-start.2
Sparse Core Ops, SparseCore 0:
  46.5 26.2 reduce-scatter.1
where the time goes:
time: 80 us; the launch traced here: 79.7 us
  waiting for transfers between devices  26.4 us (33%)
  blocking collectives  18.4 us (23%)
  local copies, waits for them, and re-layouts  15.1 us (19%)
  between operations  14.2 us (18%)
  matrix products  3.28 us (4%)
  other arithmetic  2.31 us (3%)
    reduce_scatter x1, waiting for transfers between devices, local(): lax.psum_scatter(partial_value, 'row', scatter_dimension=1, tiled=True)  26.4 us
    all_gather x1, blocking collectives, local(): gathered = lax.all_gather(adjoint, 'col', axis=1, tiled=True)  18.4 us
    gather x1, local copies, waits for them, and re-layouts, local(): jnp.take(gathered, panel_order[0], axis=1)  12.1 us
    dot_general x1, matrix products, local(): jnp.einsum('ackr,acrb->kcb', projected, right_factor, preferred_element_t...  2.29 us
  transfers between devices with their start and end apart: 1, of which 1 were waited for; matrix products, arithmetic and copies ran while one was open for 0% of the time, Pallas kernels for 0%

commit v1 on v0

v1 whole, which is shorter than its diff:
```python
import functools

import jax
import jax.numpy as jnp
from jax import lax
from jax.experimental import pallas as pl
from jax.experimental.pallas import tpu as pltpu
from jax.sharding import PartitionSpec as P

F32 = jnp.float32
BF16 = jnp.bfloat16
VMEM = pl.BlockSpec(memory_space=pltpu.VMEM)
SMEM = pl.BlockSpec(memory_space=pltpu.SMEM)


def reorder_tile(tile, ids_ref, first_id, order_ref, units_ref, start):
    width = order_ref.shape[2]
    rows = start.shape[0]
    order = order_ref[tile]
    low = jnp.bitwise_and(order, width - 1)
    high = jnp.right_shift(order, width.bit_length() - 1)
    onehot = jnp.where(lax.broadcasted_iota(jnp.int32, (width, width), 0) == low, 1.0, 0.0).astype(BF16)
    total = start
    slots = units_ref.shape[0] // rows
    for half in range(units_ref.shape[1] // width):
        picked = jnp.dot(units_ref[:, half * width : (half + 1) * width], onehot, preferred_element_type=F32)
        for slot in range(slots):
            own = ids_ref[first_id + half * slots + slot]
            total = jnp.where(high == own, picked[slot * rows : (slot + 1) * rows], total)
    return total


def reorder_kernel(ids_ref, order_ref, units_ref, out_ref):
    tiles, rows, width = out_ref.shape

    def one(tile, carry):
        out_ref[tile] = reorder_tile(tile, ids_ref, 0, order_ref, units_ref, jnp.zeros((rows, width), F32)).astype(BF16)
        return carry

    lax.fori_loop(0, tiles, one, 0, unroll=2)


def main_kernel(
    first_id, ids_ref, rank_ref, index_ref, count_ref, order_ref, units_ref, part_ref, left_ref, right_ref, near_ref,
    out_ref, *refs
):
    *send_refs, x_ref, wide_ref, sum_ref = refs
    tiles, rows, width = x_ref.shape
    _, cols, rank_most, _ = left_ref.shape
    lanes = cols * rank_most

    def one(tile, carry):
        x = reorder_tile(tile, ids_ref, first_id, order_ref, units_ref, part_ref[tile].astype(F32)).astype(BF16)
        x_ref[tile] = x
        left = left_ref[tile].reshape(lanes, width)
        projected = lax.dot_general(x, left, (((1,), (1,)), ((), ())), preferred_element_type=F32)
        lane = lax.broadcasted_iota(jnp.int32, (1, lanes), 1)
        for col in range(cols):
            keep = (lane >= col * rank_most) & (lane < col * rank_most + rank_ref[tile, col])
            wide_ref[tile, col * rows : (col + 1) * rows, :] = jnp.where(keep, projected, 0.0).astype(BF16)
        return carry

    lax.fori_loop(0, tiles, one, 0, unroll=2)
    wide = jnp.concatenate([wide_ref[tile] for tile in range(tiles)], axis=1)
    right = right_ref[...].reshape(tiles * lanes, width)
    far = jnp.dot(wide, right, preferred_element_type=F32)
    pieces = width // 128
    for col in range(cols):
        for piece in range(pieces):
            sum_ref[col * pieces + piece] = far[col * rows : (col + 1) * rows, piece * 128 : (piece + 1) * 128]
    for slot in range(near_ref.shape[0]):
        product = jnp.dot(x_ref[index_ref[0, slot]], near_ref[slot], preferred_element_type=F32)
        product = jnp.where(slot < count_ref[0], product, 0.0)
        at = index_ref[1, slot] * pieces
        for piece in range(pieces):
            sum_ref[at + piece] += product[:, piece * 128 : (piece + 1) * 128]
    row = count_ref[1]
    blocks = out_ref.shape[1] // 128
    for block in range(blocks):
        out_ref[:, block * 128 : (block + 1) * 128] = sum_ref[row * blocks + block]
    for distance, send_ref in enumerate(send_refs, 1):
        to = jnp.bitwise_xor(row, distance)
        for block in range(blocks):
            send_ref[:, block * 128 : (block + 1) * 128] = sum_ref[to * blocks + block].astype(send_ref.dtype)


def local(sizes, adjoint, panel_order, left, right, tile_ranks, near_blocks, near_index, near_count):
    n_row, n_col = sizes
    rows, own_cols = adjoint.shape
    tiles, cols, rank_most, width = left.shape
    order = panel_order.reshape(tiles, 1, width)
    row, col = lax.axis_index("row"), lax.axis_index("col")
    swap = lambda x, axis, n, d: lax.ppermute(x, axis, [(i, i ^ d) for i in range(n)])
    if own_cols % width == 0:
        slots, halves = n_col // 2, own_cols // width
        mine = jnp.concatenate([adjoint] + [swap(adjoint, "col", n_col, d) for d in range(2, n_col, 2)], 0)
        theirs = swap(mine, "col", n_col, 1)
        near = jnp.arange(slots, dtype=jnp.int32) * 2
        ids = jnp.concatenate(
            [jnp.bitwise_xor(near + core, col) * halves + half for core in range(2) for half in range(halves)]
        ).astype(jnp.int32)
    else:
        slots, halves = 1, tiles // 2
        mine, theirs = jnp.split(lax.all_gather(adjoint, "col", axis=1, tiled=True), 2, axis=1)
        ids = jnp.arange(tiles, dtype=jnp.int32)
    part = pl.pallas_call(
        reorder_kernel,
        out_shape=jax.ShapeDtypeStruct((tiles, rows, width), BF16),
        in_specs=[SMEM, VMEM, VMEM],
        out_specs=VMEM,
        cost_estimate=pl.CostEstimate(flops=rows * tiles * width * width * slots * halves * 2, bytes_accessed=0, transcendentals=0),
        compiler_params=pltpu.CompilerParams(vmem_limit_bytes=16 << 20),
        name="reorder",
    )(ids, order, mine)
    out_cols = cols * width // n_row
    counts = jnp.stack([near_count[0, 0], row.astype(jnp.int32)])
    out, *sends = pl.pallas_call(
        functools.partial(main_kernel, slots * halves),
        out_shape=[jax.ShapeDtypeStruct((rows, out_cols), F32)]
        + [jax.ShapeDtypeStruct((rows, out_cols), BF16)] * (n_row - 1),
        in_specs=[SMEM] * 4 + [VMEM] * 6,
        out_specs=[VMEM] * n_row,
        scratch_shapes=[
            pltpu.VMEM((tiles, rows, width), BF16),
            pltpu.VMEM((tiles, cols * rows, cols * rank_most), BF16),
            pltpu.VMEM((cols * width // 128, rows, 128), F32),
        ],
        compiler_params=pltpu.CompilerParams(vmem_limit_bytes=32 << 20),
        name="apply",
    )(ids, tile_ranks, near_index[0, 0], counts, order, theirs, part, left, right, near_blocks[0, 0])
    for distance, send in enumerate(sends, 1):
        out = out + swap(send, "row", n_row, distance).astype(F32)
    return out


def solution(mesh):
    placed = (
        P(None, ("row", "col")),
        P("row", None),
        P("row", "col", None, None),
        P("row", "col", None, None),
        P("row", "col"),
        P("row", "col", None, None, None),
        P("row", "col", None, None),
        P("row", "col"),
    )
    sizes = (mesh.shape["row"], mesh.shape["col"])
    return jax.shard_map(
        functools.partial(local, sizes), mesh=mesh, in_specs=placed, out_specs=P(None, ("col", "row")), check_vma=False
    )
```

time: 80 us -> 31.9 us (0.40)
  blocking collectives: 18.4 us -> 0 us
  waiting for transfers between devices: 26.4 us -> 9.34 us
  between operations: 14.2 us -> 0.77 us
  local copies, waits for them, and re-layouts: 15.1 us -> 2.17 us
  Pallas kernels: 0 us -> 9.31 us
  starting transfers between devices: 0.01 us -> 9.24 us
  matrix products: 3.28 us -> 0 us
  other arithmetic: 2.31 us -> 0.86 us
    reduce_scatter x1 -> x0, waiting for transfers between devices: 26.4 us -> none  [local(): lax.psum_scatter(partial_value, 'row', scatter_dimension=1, tiled=True)]
    all_gather x1 -> x0, blocking collectives: 18.4 us -> none  [local(): gathered = lax.all_gather(adjoint, 'col', axis=1, tiled=True)]
    gather x2 -> x0, local copies, waits for them, and re-layouts: 12.8 us -> none  [the longest x1 12.1 us: local(): jnp.take(gathered, panel_order[0], axis=1)]
    ppermute x0 -> x7, waiting for transfers between devices: none -> 9.34 us  [local(): lax.ppermute(x, axis, [(i, i ^ d) for i in range(n)])]
    pallas_call x0 -> x2, Pallas kernels: none -> 9.31 us  [the longest x1 6.19 us: local(): pl.pallas_call(functools.partial(main_kernel, slots * halves), out_shape=...]
    ppermute x0 -> x7, starting transfers between devices: none -> 9.24 us  [local(): lax.ppermute(x, axis, [(i, i ^ d) for i in range(n)])]
    dot_general x3 -> x0, matrix products: 3.28 us -> none  [the longest x1 2.29 us: local(): jnp.einsum('ackr,acrb->kcb', projected, right_factor, preferred_element_t...]
    select_n x3 -> x0, other arithmetic: 1.52 us -> none  [the longest x1 0.78 us: local(): picked = tiled[:, row_list, :]]
  transfers between devices with their start and end apart: 1 -> 7, of which waited for: 1 -> 5; matrix products, arithmetic and copies ran while one was open for 0% -> 4% of each run, Pallas kernels for 0% -> 10%
where the time goes in v1:
time: 31.9 us; the launch traced here: 31.7 us
  waiting for transfers between devices  9.34 us (29%)
  Pallas kernels  9.31 us (29%)
  starting transfers between devices  9.24 us (29%)
  local copies, waits for them, and re-layouts  2.17 us (7%)
  other arithmetic  0.86 us (3%)
  between operations  0.77 us (2%)
    ppermute x7, waiting for transfers between devices, local(): lax.ppermute(x, axis, [(i, i ^ d) for i in range(n)])  9.34 us
    ppermute x7, starting transfers between devices, local(): lax.ppermute(x, axis, [(i, i ^ d) for i in range(n)])  9.24 us
    pallas_call x1, Pallas kernels, local(): pl.pallas_call(functools.partial(main_kernel, slots * halves), out_shape=...  6.19 us
    pallas_call x1, Pallas kernels, local(): pl.pallas_call(reorder_kernel, out_shape=jax.ShapeDtypeStruct((tiles, row...  3.13 us
    unnamed x16, local copies, waits for them, and re-layouts  2.17 us
    add x1, other arithmetic, local(): out = out + swap(send, 'row', n_row, distance).astype(F32)  0.68 us
  transfers between devices with their start and end apart: 7, of which 5 were waited for; matrix products, arithmetic and copies ran while one was open for 4% of the time, Pallas kernels for 10%

profile of v1, /device:TPU:0, one launch (start us, length us, event | category | flops | bytes accessed | tf_op | source)
XLA Modules:
  0.0 31.7 jit_solution(16240658440629417430)
XLA Ops:
  0.0 4.0 %collective-permute-start.1 = (bf16[64,512]{1,0:T(8,128)(2,1)}, bf16[64,512]{1,0:T(8,128)(2,1)S(1)}, u32[]{:S(2)}, u32[]{:S(2)}) collective-permute-start(bf16[64,512]{1,0:T(8,128)(2,1)} %param.8), channel_id=1, source_target_pairs={{0,4},{1,5},{2,6},{3,7},{4,0},{5,1},{6,2},{7,3},{8,12},{9,13},{10,... | collective-permute-start | bytes 196616 | tf_op jit(solution)/shard_map/ppermute | solution.py:93
  4.0 1.6 %collective-permute-start = (bf16[64,512]{1,0:T(8,128)(2,1)}, bf16[64,512]{1,0:T(8,128)(2,1)S(1)}, u32[]{:S(2)}, u32[]{:S(2)}) collective-permute-start(bf16[64,512]{1,0:T(8,128)(2,1)} %param.8), channel_id=1, source_target_pairs={{0,2},{1,3},{2,0},{3,1},{4,6},{5,7},{6,4},{7,5},{8,10},{9,11},{10,... | collective-permute-start | bytes 196616 | tf_op jit(solution)/shard_map/ppermute | solution.py:93
  5.6 0.9 %constant_dynamic-update-slice_fusion.3 = bf16[256,512]{1,0:T(8,128)(2,1)S(1)} fusion(bf16[64,512]{1,0:T(8,128)(2,1)} %param.8), kind=kLoop, calls=%fused_computation.4 | loop fusion | bytes 131072
  7.2 1.3 %collective-permute-done = bf16[64,512]{1,0:T(8,128)(2,1)S(1)} collective-permute-done((bf16[64,512]{1,0:T(8,128)(2,1)}, bf16[64,512]{1,0:T(8,128)(2,1)S(1)}, u32[]{:S(2)}, u32[]{:S(2)}) %collective-permute-start) | collective-permute-done | bytes 65568 | tf_op jit(solution)/shard_map/ppermute | solution.py:93
  8.5 0.0 collective-permute-done.1
  8.5 3.3 %collective-permute-done.2 = bf16[64,512]{1,0:T(8,128)(2,1)S(1)} collective-permute-done((bf16[64,512]{1,0:T(8,128)(2,1)}, bf16[64,512]{1,0:T(8,128)(2,1)S(1)}, u32[]{:S(2)}, u32[]{:S(2)}) %collective-permute-start.2) | collective-permute-done | bytes 65568 | tf_op jit(solution)/shard_map/ppermute | solution.py:93
  11.9 0.0 copy-start.3
  11.9 0.1 collective-permute-start.3
  12.0 0.1 pad_add_fusion.1.count_ref
  12.1 0.5 %copy-done.5 = s32[16,8]{0,1:T(8,128)S(1)} copy-done((s32[16,8]{0,1:T(8,128)S(1)}, s32[16,8]{0,1:T(8,128)}, u32[]{:S(2)}) %copy-start.5) | copy-done | bytes 536
  12.6 0.1 copy.9.rank_ref
  12.6 0.1 pad_add_fusion.ids_ref
  12.7 0.0 copy-start.2
  12.7 3.1 %reorder.1.part_ref = bf16[16,64,256]{2,1,0:T(8,128)(2,1)S(1)} custom-call(s32[16]{0:T(128)S(1)} %pad_add_fusion.ids_ref, s32[16,1,256]{2,1,0:T(1,128)S(1)} %bitcast.7, bf16[256,512]{1,0:T(8,128)(2,1)S(1)} %constant_dynamic-update-slice_fusion.units_ref), custom_call_target="tpu_custom_call" | custom-call | flops 1073741824 | tf_op jit(solution)/shard_map/reorder/pallas_call | solution.py:106
  15.9 0.0 copy-start.4
  15.9 0.6 %copy-done.4 = s32[1,1,2,8]{3,2,1,0:T(2,128)S(1)} copy-done((s32[1,1,2,8]{3,2,1,0:T(2,128)S(1)}, s32[1,1,2,8]{3,2,1,0:T(2,128)}, u32[]{:S(2)}) %copy-start.4) | copy-done | bytes 88
  16.6 6.2 %apply.1 = (f32[64,512]{1,0:T(8,128)S(1)}, bf16[64,512]{1,0:T(8,128)(2,1)S(1)}, bf16[64,512]{1,0:T(8,128)(2,1)S(1)}, bf16[64,512]{1,0:T(8,128)(2,1)S(1)}) custom-call(s32[16]{0:T(128)S(1)} %pad_add_fusion.ids_ref, s32[16,8]{1,0:T(8,128)S(1)} %copy.9.rank_ref, s32[2,8]{1,0:T(2,128)S(1)} %bitcast.9, s32[2]{0:T(128)S(1)} %pad_add_fusion.1.count_ref, ...), custom_call_target="tpu_custom_call" | custom-call | tf_op jit(solution)/shard_map/apply/pallas_call | solution.py:117
  22.8 1.6 %collective-permute-start.4 = (bf16[64,512]{1,0:T(8,128)(2,1)S(1)}, bf16[64,512]{1,0:T(8,128)(2,1)S(1)}, u32[]{:S(2)}, u32[]{:S(2)}) collective-permute-start(bf16[64,512]{1,0:T(8,128)(2,1)S(1)} %get-tuple-element.10), channel_id=1, source_target_pairs={{0,8},{8,0},{16,24},{24,16},{1,9},{9,1},{17,25},{25,17},{2,10},{10... | collective-permute-start | bytes 196616 | tf_op jit(solution)/shard_map/ppermute | solution.py:93
  24.3 1.5 %collective-permute-start.5 = (bf16[64,512]{1,0:T(8,128)(2,1)S(1)}, bf16[64,512]{1,0:T(8,128)(2,1)S(1)}, u32[]{:S(2)}, u32[]{:S(2)}) collective-permute-start(bf16[64,512]{1,0:T(8,128)(2,1)S(1)} %get-tuple-element.11), channel_id=1, source_target_pairs={{0,16},{8,24},{16,0},{24,8},{1,17},{9,25},{17,1},{25,9},{2,18},{10... | collective-permute-start | bytes 196616 | tf_op jit(solution)/shard_map/ppermute | solution.py:93
  25.8 0.5 %collective-permute-start.6 = (bf16[64,512]{1,0:T(8,128)(2,1)S(1)}, bf16[64,512]{1,0:T(8,128)(2,1)S(1)}, u32[]{:S(2)}, u32[]{:S(2)}) collective-permute-start(bf16[64,512]{1,0:T(8,128)(2,1)S(1)} %get-tuple-element.12), channel_id=1, source_target_pairs={{0,24},{8,16},{16,8},{24,0},{1,25},{9,17},{17,9},{25,1},{2,26},{10... | collective-permute-start | bytes 196616 | tf_op jit(solution)/shard_map/ppermute | solution.py:93
  26.3 0.8 %collective-permute-done.4 = bf16[64,512]{1,0:T(8,128)(2,1)S(1)} collective-permute-done((bf16[64,512]{1,0:T(8,128)(2,1)S(1)}, bf16[64,512]{1,0:T(8,128)(2,1)S(1)}, u32[]{:S(2)}, u32[]{:S(2)}) %collective-permute-start.4) | collective-permute-done | bytes 65568 | tf_op jit(solution)/shard_map/ppermute | solution.py:93
  27.1 1.5 %collective-permute-done.5 = bf16[64,512]{1,0:T(8,128)(2,1)S(1)} collective-permute-done((bf16[64,512]{1,0:T(8,128)(2,1)S(1)}, bf16[64,512]{1,0:T(8,128)(2,1)S(1)}, u32[]{:S(2)}, u32[]{:S(2)}) %collective-permute-start.5) | collective-permute-done | bytes 65568 | tf_op jit(solution)/shard_map/ppermute | solution.py:93
  28.6 2.4 %collective-permute-done.6 = bf16[64,512]{1,0:T(8,128)(2,1)S(1)} collective-permute-done((bf16[64,512]{1,0:T(8,128)(2,1)S(1)}, bf16[64,512]{1,0:T(8,128)(2,1)S(1)}, u32[]{:S(2)}, u32[]{:S(2)}) %collective-permute-start.6) | collective-permute-done | bytes 65568 | tf_op jit(solution)/shard_map/ppermute | solution.py:93
  31.0 0.7 %convert_add_fusion = f32[64,512]{1,0:T(8,128)} fusion(bf16[64,512]{1,0:T(8,128)(2,1)S(1)} %collective-permute-done.6, bf16[64,512]{1,0:T(8,128)(2,1)S(1)} %collective-permute-done.5, f32[64,512]{1,0:T(8,128)S(1)} %get-tuple-element.9, bf16[64,512]{1,0:T(8,128)(2,1)S(1)} %collective-permute-done.4), kind=kLoop, calls=%fused_computation | loop fusion | flops 196608 | bytes 458752 | tf_op jit(solution)/shard_map/add | solution.py:132
  (14 shorter events, 0.1 us)
Async XLA Ops:
  0.0 8.5 %collective-permute-start.1 = (bf16[64,512]{1,0:T(8,128)(2,1)}, bf16[64,512]{1,0:T(8,128)(2,1)S(1)}, u32[]{:S(2)}, u32[]{:S(2)}) collective-permute-start(bf16[64,512]{1,0:T(8,128)(2,1)} %param.8), channel_id=1, source_target_pairs={{0,4},{1,5},{2,6},{3,7},{4,0},{5,1},{6,2},{7,3},{8,12},{9,13},{10,... | collective-permute-start | bytes 196616 | tf_op jit(solution)/shard_map/ppermute | solution.py:93
  4.0 4.5 %collective-permute-start = (bf16[64,512]{1,0:T(8,128)(2,1)}, bf16[64,512]{1,0:T(8,128)(2,1)S(1)}, u32[]{:S(2)}, u32[]{:S(2)}) collective-permute-start(bf16[64,512]{1,0:T(8,128)(2,1)} %param.8), channel_id=1, source_target_pairs={{0,2},{1,3},{2,0},{3,1},{4,6},{5,7},{6,4},{7,5},{8,10},{9,11},{10,... | collective-permute-start | bytes 196616 | tf_op jit(solution)/shard_map/ppermute | solution.py:93
  5.6 6.3 %collective-permute-start.2 = (bf16[64,512]{1,0:T(8,128)(2,1)}, bf16[64,512]{1,0:T(8,128)(2,1)S(1)}, u32[]{:S(2)}, u32[]{:S(2)}) collective-permute-start(bf16[64,512]{1,0:T(8,128)(2,1)} %param.8), channel_id=1, source_target_pairs={{0,6},{1,7},{2,4},{3,5},{4,2},{5,3},{6,0},{7,1},{8,14},{9,15},{10,... | collective-permute-start | bytes 196616 | tf_op jit(solution)/shard_map/ppermute | solution.py:93
  11.9 0.7 %copy-start.5 = (s32[16,8]{0,1:T(8,128)S(1)}, s32[16,8]{0,1:T(8,128)}, u32[]{:S(2)}) copy-start(s32[16,8]{0,1:T(8,128)} %param.12) | copy-start | bytes 1540
  11.9 0.8 %copy-start.3 = (s32[1,4096]{1,0:T(1,128)S(1)}, s32[1,4096]{1,0:T(1,128)}, u32[]{:S(2)}) copy-start(s32[1,4096]{1,0:T(1,128)} %param.9) | copy-start | bytes 49156
  11.9 4.0 %collective-permute-start.3 = (bf16[256,512]{1,0:T(8,128)(2,1)S(1)}, bf16[256,512]{1,0:T(8,128)(2,1)S(1)}, u32[]{:S(2)}, u32[]{:S(2)}) collective-permute-start(bf16[256,512]{1,0:T(8,128)(2,1)S(1)} %constant_dynamic-update-slice_fusion.units_ref), channel_id=1, source_target_pairs={{0,1},{1,0},{2,3},{3,2},{4,5},{5,4},{6,7},{7,6},{8,9},{9,8},{10,11... | collective-permute-start | bytes 786440 | tf_op jit(solution)/shard_map/ppermute | solution.py:93
  12.7 3.2 %copy-start = (bf16[16,8,16,256]{3,2,1,0:T(8,128)(2,1)S(1)}, bf16[16,8,16,256]{3,2,1,0:T(8,128)(2,1)}, u32[]{:S(2)}) copy-start(bf16[16,8,16,256]{3,2,1,0:T(8,128)(2,1)} %left_ref.1) | copy-start | bytes 3145732
  12.7 3.2 %copy-start.1 = (bf16[16,8,16,256]{3,2,1,0:T(8,128)(2,1)S(1)}, bf16[16,8,16,256]{3,2,1,0:T(8,128)(2,1)}, u32[]{:S(2)}) copy-start(bf16[16,8,16,256]{3,2,1,0:T(8,128)(2,1)} %right_ref.1) | copy-start | bytes 3145732
  12.7 3.2 %copy-start.2 = (bf16[1,1,8,256,256]{4,3,2,1,0:T(8,128)(2,1)S(1)}, bf16[1,1,8,256,256]{4,3,2,1,0:T(8,128)(2,1)}, u32[]{:S(2)}) copy-start(bf16[1,1,8,256,256]{4,3,2,1,0:T(8,128)(2,1)} %param.13) | copy-start | bytes 3145732
  15.9 0.7 %copy-start.4 = (s32[1,1,2,8]{3,2,1,0:T(2,128)S(1)}, s32[1,1,2,8]{3,2,1,0:T(2,128)}, u32[]{:S(2)}) copy-start(s32[1,1,2,8]{3,2,1,0:T(2,128)} %param.14) | copy-start | bytes 196
  22.8 4.3 %collective-permute-start.4 = (bf16[64,512]{1,0:T(8,128)(2,1)S(1)}, bf16[64,512]{1,0:T(8,128)(2,1)S(1)}, u32[]{:S(2)}, u32[]{:S(2)}) collective-permute-start(bf16[64,512]{1,0:T(8,128)(2,1)S(1)} %get-tuple-element.10), channel_id=1, source_target_pairs={{0,8},{8,0},{16,24},{24,16},{1,9},{9,1},{17,25},{25,17},{2,10},{10... | collective-permute-start | bytes 196616 | tf_op jit(solution)/shard_map/ppermute | solution.py:93
  24.3 4.3 %collective-permute-start.5 = (bf16[64,512]{1,0:T(8,128)(2,1)S(1)}, bf16[64,512]{1,0:T(8,128)(2,1)S(1)}, u32[]{:S(2)}, u32[]{:S(2)}) collective-permute-start(bf16[64,512]{1,0:T(8,128)(2,1)S(1)} %get-tuple-element.11), channel_id=1, source_target_pairs={{0,16},{8,24},{16,0},{24,8},{1,17},{9,25},{17,1},{25,9},{2,18},{10... | collective-permute-start | bytes 196616 | tf_op jit(solution)/shard_map/ppermute | solution.py:93
  25.8 5.2 %collective-permute-start.6 = (bf16[64,512]{1,0:T(8,128)(2,1)S(1)}, bf16[64,512]{1,0:T(8,128)(2,1)S(1)}, u32[]{:S(2)}, u32[]{:S(2)}) collective-permute-start(bf16[64,512]{1,0:T(8,128)(2,1)S(1)} %get-tuple-element.12), channel_id=1, source_target_pairs={{0,24},{8,16},{16,8},{24,0},{1,25},{9,17},{17,9},{25,1},{2,26},{10... | collective-permute-start | bytes 196616 | tf_op jit(solution)/shard_map/ppermute | solution.py:93

commit v2 on v1

v2 whole, which is shorter than its diff:
```python
import functools

import jax
import jax.numpy as jnp
from jax import lax
from jax.experimental import pallas as pl
from jax.experimental.pallas import tpu as pltpu
from jax.sharding import PartitionSpec as P

F32 = jnp.float32
BF16 = jnp.bfloat16
VMEM = pl.BlockSpec(memory_space=pltpu.VMEM)
SMEM = pl.BlockSpec(memory_space=pltpu.SMEM)
ROW, COL, COUNT, INDEX = 0, 1, 2, 3


def slab_blocks(meta_ref, slabs, width):
    blocks = []
    for ref, distances in slabs:
        halves = ref.shape[1] // width
        for half in range(halves):
            ids = [half if d is None else jnp.bitwise_xor(meta_ref[COL], d) * halves + half for d in distances]
            blocks.append((ref, half, ids))
    return blocks


def reorder_tile(tile, order_ref, blocks, total):
    rows, width = total.shape
    order = order_ref[tile]
    low = jnp.bitwise_and(order, width - 1)
    high = jnp.right_shift(order, width.bit_length() - 1)
    onehot = jnp.where(lax.broadcasted_iota(jnp.int32, (width, width), 0) == low, 1.0, 0.0).astype(BF16)
    for ref, half, ids in blocks:
        picked = jnp.dot(ref[:, half * width : (half + 1) * width], onehot, preferred_element_type=F32)
        for slot, own in enumerate(ids):
            total = jnp.where(high == own, picked[slot * rows : (slot + 1) * rows], total)
    return total


def reorder_kernel(distances, first, meta_ref, order_ref, *refs):
    out_ref = refs[len(distances) + (not first)]
    for spare_ref in refs[len(distances) + (not first) + 1 :]:
        spare_ref[...] = jnp.zeros(spare_ref.shape, spare_ref.dtype)
    slabs = list(zip(refs, distances))
    tiles, rows, width = out_ref.shape
    blocks = slab_blocks(meta_ref, slabs, width)
    for tile in range(tiles):
        total = jnp.zeros((rows, width), F32) if first else refs[len(distances)][tile].astype(F32)
        out_ref[tile] = reorder_tile(tile, order_ref, blocks, total).astype(BF16)


def main_kernel(distances, meta_ref, order_ref, left_ref, right_ref, near_ref, part_ref, *refs):
    slabs = list(zip(refs, distances))
    out_ref, *send_refs, x_ref, wide_ref, sum_ref = refs[len(distances) :]
    tiles, rows, width = x_ref.shape
    _, cols, rank_most, _ = left_ref.shape
    slot_most = near_ref.shape[0]
    lanes = cols * rank_most
    blocks = slab_blocks(meta_ref, slabs, width)
    lane = lax.broadcasted_iota(jnp.int32, (1, lanes), 1)
    for tile in range(tiles):
        x = reorder_tile(tile, order_ref, blocks, part_ref[tile].astype(F32)).astype(BF16)
        x_ref[tile] = x
        left = left_ref[tile].reshape(lanes, width)
        projected = lax.dot_general(x, left, (((1,), (1,)), ((), ())), preferred_element_type=F32)
        for col in range(cols):
            rank = meta_ref[INDEX + 2 * slot_most + tile * cols + col]
            keep = (lane >= col * rank_most) & (lane < col * rank_most + rank)
            wide_ref[tile, col * rows : (col + 1) * rows, :] = jnp.where(keep, projected, 0.0).astype(BF16)
    wide = jnp.concatenate([wide_ref[tile] for tile in range(tiles)], axis=1)
    right = right_ref[...].reshape(tiles * lanes, width)
    far = jnp.dot(wide, right, preferred_element_type=F32)
    pieces = width // 128
    for col in range(cols):
        for piece in range(pieces):
            sum_ref[col * pieces + piece] = far[col * rows : (col + 1) * rows, piece * 128 : (piece + 1) * 128]
    for slot in range(slot_most):
        product = jnp.dot(x_ref[meta_ref[INDEX + slot]], near_ref[slot], preferred_element_type=F32)
        product = jnp.where(slot < meta_ref[COUNT], product, 0.0)
        at = meta_ref[INDEX + slot_most + slot] * pieces
        for piece in range(pieces):
            sum_ref[at + piece] += product[:, piece * 128 : (piece + 1) * 128]
    row = meta_ref[ROW]
    parts = out_ref.shape[1] // 128
    for part in range(parts):
        out_ref[:, part * 128 : (part + 1) * 128] = sum_ref[row * parts + part]
    for distance, send_ref in enumerate(send_refs, 1):
        to = jnp.bitwise_xor(row, distance)
        for part in range(parts):
            send_ref[:, part * 128 : (part + 1) * 128] = sum_ref[to * parts + part].astype(send_ref.dtype)


def local(sizes, adjoint, panel_order, left, right, tile_ranks, near_blocks, near_index, near_count):
    n_row, n_col = sizes
    rows, own_cols = adjoint.shape
    tiles, cols, rank_most, width = left.shape
    order = panel_order.reshape(tiles, 1, width)
    swap = lambda x, axis, n, d: lax.ppermute(x, axis, [(i, i ^ d) for i in range(n)])
    place = jnp.stack([lax.axis_index("row"), lax.axis_index("col"), near_count[0, 0]]).astype(jnp.int32)
    meta = jnp.concatenate([place, near_index.reshape(-1), tile_ranks.reshape(-1)])

    def reorder(slabs, distances, part=None, spare=0):
        slots = sum(slab.shape[0] * slab.shape[1] for slab in slabs)
        return pl.pallas_call(
            functools.partial(reorder_kernel, distances, part is None),
            out_shape=[jax.ShapeDtypeStruct((tiles, rows, width), BF16)]
            + ([jax.ShapeDtypeStruct((spare, own_cols), BF16)] if spare else []),
            in_specs=[SMEM] + [VMEM] * (1 + len(slabs) + (part is not None)),
            out_specs=[VMEM] * (1 + (spare > 0)),
            cost_estimate=pl.CostEstimate(flops=2 * slots * tiles * width, bytes_accessed=0, transcendentals=0),
            compiler_params=pltpu.CompilerParams(vmem_limit_bytes=16 << 20),
            name="reorder",
        )(meta, order, *slabs, *([] if part is None else [part]))

    if own_cols % width == 0:
        far_off = [n_col - 2] + list(range(2, n_col - 2, 2))
        beside = swap(adjoint, "col", n_col, 1)
        near_part, got = reorder([adjoint, beside], [[0], [1]], spare=len(far_off) * rows)
        for at, d in enumerate(far_off):
            got = lax.dynamic_update_slice_in_dim(got, swap(adjoint, "col", n_col, d), at * rows, 0)
        last, last_off = [swap(got, "col", n_col, 1)], [[d ^ 1 for d in far_off]]
        (part,) = reorder([got], [far_off], near_part)
    else:
        part = jnp.zeros((tiles, rows, width), BF16)
        last, last_off = [lax.all_gather(adjoint, "col", axis=1, tiled=True)], [[None]]
    out_cols = cols * width // n_row
    out, *sends = pl.pallas_call(
        functools.partial(main_kernel, last_off),
        out_shape=[jax.ShapeDtypeStruct((rows, out_cols), F32)]
        + [jax.ShapeDtypeStruct((rows, out_cols), BF16)] * (n_row - 1),
        in_specs=[SMEM] + [VMEM] * (5 + len(last)),
        out_specs=[VMEM] * n_row,
        scratch_shapes=[
            pltpu.VMEM((tiles, rows, width), BF16),
            pltpu.VMEM((tiles, cols * rows, cols * rank_most), BF16),
            pltpu.VMEM((cols * width // 128, rows, 128), F32),
        ],
        compiler_params=pltpu.CompilerParams(vmem_limit_bytes=32 << 20),
        name="apply",
    )(meta, order, left, right, near_blocks[0, 0], part, *last)
    for distance, send in enumerate(sends, 1):
        out = out + swap(send, "row", n_row, distance).astype(F32)
    return out


def solution(mesh):
    placed = (
        P(None, ("row", "col")),
        P("row", None),
        P("row", "col", None, None),
        P("row", "col", None, None),
        P("row", "col"),
        P("row", "col", None, None, None),
        P("row", "col", None, None),
        P("row", "col"),
    )
    sizes = (mesh.shape["row"], mesh.shape["col"])
    return jax.shard_map(
        functools.partial(local, sizes), mesh=mesh, in_specs=placed, out_specs=P(None, ("col", "row")), check_vma=False
    )
```

time: 31.9 us -> 26.8 us (0.84)
  waiting for transfers between devices: 9.34 us -> 5.89 us
  Pallas kernels: 9.31 us -> 8.27 us
  local copies, waits for them, and re-layouts: 2.17 us -> 1.68 us
    ppermute x7 -> x8, waiting for transfers between devices: 9.34 us -> 5.89 us  [local(): lax.ppermute(x, axis, [(i, i ^ d) for i in range(n)])]
    pallas_call x2 -> x3, Pallas kernels: 9.31 us -> 8.27 us  [the longest x1 4.5 us: local(): pl.pallas_call(functools.partial(main_kernel, last_off), out_shape=[jax.S...]
    unnamed x16 -> x15, local copies, waits for them, and re-layouts: 2.17 us -> 1.42 us
    ppermute x7 -> x8, starting transfers between devices: 9.24 us -> 9.24 us  [local(): lax.ppermute(x, axis, [(i, i ^ d) for i in range(n)])]
  transfers between devices with their start and end apart: 7 -> 8, of which waited for: 5 -> 5; matrix products, arithmetic and copies ran while one was open for 4% -> 1% of each run, Pallas kernels for 10% -> 14%
where the time goes in v2:
time: 26.8 us; the launch traced here: 26.6 us
  starting transfers between devices  9.24 us (34%)
  Pallas kernels  8.27 us (31%)
  waiting for transfers between devices  5.89 us (22%)
  local copies, waits for them, and re-layouts  1.68 us (6%)
  between operations  0.79 us (3%)
  other arithmetic  0.68 us (3%)
    ppermute x8, starting transfers between devices, local(): lax.ppermute(x, axis, [(i, i ^ d) for i in range(n)])  9.24 us
    ppermute x8, waiting for transfers between devices, local(): lax.ppermute(x, axis, [(i, i ^ d) for i in range(n)])  5.89 us
    pallas_call x1, Pallas kernels, local(): pl.pallas_call(functools.partial(main_kernel, last_off), out_shape=[jax.S...  4.5 us
    pallas_call x2, Pallas kernels, reorder(): pl.pallas_call(functools.partial(reorder_kernel, distances, part is None)...  3.76 us
    unnamed x15, local copies, waits for them, and re-layouts  1.42 us
    add x1, other arithmetic, local(): out = out + swap(send, 'row', n_row, distance).astype(F32)  0.68 us
  transfers between devices with their start and end apart: 8, of which 5 were waited for; matrix products, arithmetic and copies ran while one was open for 1% of the time, Pallas kernels for 14%

profile of v2, /device:TPU:0, one launch (start us, length us, event | category | flops | bytes accessed | tf_op | source)
XLA Modules:
  0.0 26.6 jit_solution(6924796216340934770)
XLA Ops:
  0.0 0.5 %collective-permute-start = (bf16[64,512]{1,0:T(8,128)(2,1)}, bf16[64,512]{1,0:T(8,128)(2,1)S(1)}, u32[]{:S(2)}, u32[]{:S(2)}) collective-permute-start(bf16[64,512]{1,0:T(8,128)(2,1)} %refs_0_.1), channel_id=1, source_target_pairs={{0,1},{1,0},{2,3},{3,2},{4,5},{5,4},{6,7},{7,6},{8,9},{9,8},{10,11... | collective-permute-start | bytes 196616 | tf_op jit(solution)/shard_map/ppermute | solution.py:98
  0.5 4.6 %collective-permute-start.1 = (bf16[64,512]{1,0:T(8,128)(2,1)}, bf16[64,512]{1,0:T(8,128)(2,1)S(1)}, u32[]{:S(2)}, u32[]{:S(2)}) collective-permute-start(bf16[64,512]{1,0:T(8,128)(2,1)} %refs_0_.1), channel_id=1, source_target_pairs={{0,6},{1,7},{2,4},{3,5},{4,2},{5,3},{6,0},{7,1},{8,14},{9,15},{10,... | collective-permute-start | bytes 196616 | tf_op jit(solution)/shard_map/ppermute | solution.py:98
  5.1 0.6 %collective-permute-start.2 = (bf16[64,512]{1,0:T(8,128)(2,1)}, bf16[64,512]{1,0:T(8,128)(2,1)S(1)}, u32[]{:S(2)}, u32[]{:S(2)}) collective-permute-start(bf16[64,512]{1,0:T(8,128)(2,1)} %refs_0_.1), channel_id=1, source_target_pairs={{0,2},{1,3},{2,0},{3,1},{4,6},{5,7},{6,4},{7,5},{8,10},{9,11},{10,... | collective-permute-start | bytes 196616 | tf_op jit(solution)/shard_map/ppermute | solution.py:98
  6.4 0.0 copy-done.6
  6.4 0.1 reshape.9
  6.5 0.1 copy.10
  6.5 0.1 reshape.10
  6.6 0.1 concatenate.3.meta_ref
  6.7 0.5 %copy-done.3 = s32[1,4096]{1,0:T(1,128)S(1)} copy-done((s32[1,4096]{1,0:T(1,128)S(1)}, s32[1,4096]{1,0:T(1,128)}, u32[]{:S(2)}) %copy-start.3) | copy-done | bytes 16408
  7.2 0.8 %copy-done.4 = bf16[64,512]{1,0:T(8,128)(2,1)S(1)} copy-done((bf16[64,512]{1,0:T(8,128)(2,1)S(1)}, bf16[64,512]{1,0:T(8,128)(2,1)}, u32[]{:S(2)}) %copy-start.4) | copy-done | bytes 65560
  8.0 2.1 %reorder.2 = (bf16[16,64,256]{2,1,0:T(8,128)(2,1)S(1)}, bf16[192,512]{1,0:T(8,128)(2,1)S(1)}) custom-call(s32[147]{0:T(256)S(1)} %concatenate.3.meta_ref, s32[16,1,256]{2,1,0:T(1,128)S(1)} %bitcast.7, bf16[64,512]{1,0:T(8,128)(2,1)S(1)} %copy-done.4, bf16[64,512]{1,0:T(8,128)(2,1)S(1)} %collective-permute-done.refs_1_), custom_call_target="tpu_custom_call" | custom-call | flops 536870912 | tf_op jit(solution)/shard_map/reorder/pallas_call | solution.py:104
  10.2 0.1 collective-permute-done.2
  10.3 1.1 %collective-permute-done.3 = bf16[64,512]{1,0:T(8,128)(2,1)S(1)} collective-permute-done((bf16[64,512]{1,0:T(8,128)(2,1)}, bf16[64,512]{1,0:T(8,128)(2,1)S(1)}, u32[]{:S(2)}, u32[]{:S(2)}) %collective-permute-start.3) | collective-permute-done | bytes 65568 | tf_op jit(solution)/shard_map/ppermute | solution.py:98
  11.4 0.0 copy-start
  11.4 0.0 copy-start.1
  11.4 1.6 %reorder.3.part_ref = bf16[16,64,256]{2,1,0:T(8,128)(2,1)S(1)} custom-call(s32[147]{0:T(256)S(1)} %concatenate.3.meta_ref, s32[16,1,256]{2,1,0:T(1,128)S(1)} %bitcast.8, bf16[192,512]{1,0:T(8,128)(2,1)S(1)} %constant_dynamic-update-slice_fusion.refs_0_, bf16[16,64,256]{2,1,0:T(8,128)(2,1)S(1)} %get-tuple-element.12.refs_1_), custom_call_target="tpu_custom_call" | custom-call | flops 805306368 | tf_op jit(solution)/shard_map/reorder/pallas_call | solution.py:104
  13.1 4.5 %apply.1 = (f32[64,512]{1,0:T(8,128)S(1)}, bf16[64,512]{1,0:T(8,128)(2,1)S(1)}, bf16[64,512]{1,0:T(8,128)(2,1)S(1)}, bf16[64,512]{1,0:T(8,128)(2,1)S(1)}) custom-call(s32[147]{0:T(256)S(1)} %concatenate.3.meta_ref, s32[16,1,256]{2,1,0:T(1,128)S(1)} %bitcast.9, bf16[16,8,16,256]{3,2,1,0:T(8,128)(2,1)S(1)} %copy-done, bf16[16,8,16,256]{3,2,1,0:T(8,128)(2,1)S(1)} %copy-done.1, ...), custom_call_target="tpu_custom_call" | custom-call | tf_op jit(solution)/shard_map/apply/pallas_call | solution.py:127
  17.6 1.6 %collective-permute-start.5 = (bf16[64,512]{1,0:T(8,128)(2,1)S(1)}, bf16[64,512]{1,0:T(8,128)(2,1)S(1)}, u32[]{:S(2)}, u32[]{:S(2)}) collective-permute-start(bf16[64,512]{1,0:T(8,128)(2,1)S(1)} %get-tuple-element.14), channel_id=1, source_target_pairs={{0,8},{8,0},{16,24},{24,16},{1,9},{9,1},{17,25},{25,17},{2,10},{10... | collective-permute-start | bytes 196616 | tf_op jit(solution)/shard_map/ppermute | solution.py:98
  19.2 1.5 %collective-permute-start.6 = (bf16[64,512]{1,0:T(8,128)(2,1)S(1)}, bf16[64,512]{1,0:T(8,128)(2,1)S(1)}, u32[]{:S(2)}, u32[]{:S(2)}) collective-permute-start(bf16[64,512]{1,0:T(8,128)(2,1)S(1)} %get-tuple-element.15), channel_id=1, source_target_pairs={{0,16},{8,24},{16,0},{24,8},{1,17},{9,25},{17,1},{25,9},{2,18},{10... | collective-permute-start | bytes 196616 | tf_op jit(solution)/shard_map/ppermute | solution.py:98
  20.7 0.5 %collective-permute-start.7 = (bf16[64,512]{1,0:T(8,128)(2,1)S(1)}, bf16[64,512]{1,0:T(8,128)(2,1)S(1)}, u32[]{:S(2)}, u32[]{:S(2)}) collective-permute-start(bf16[64,512]{1,0:T(8,128)(2,1)S(1)} %get-tuple-element.16), channel_id=1, source_target_pairs={{0,24},{8,16},{16,8},{24,0},{1,25},{9,17},{17,9},{25,1},{2,26},{10... | collective-permute-start | bytes 196616 | tf_op jit(solution)/shard_map/ppermute | solution.py:98
  21.2 1.0 %collective-permute-done.5 = bf16[64,512]{1,0:T(8,128)(2,1)S(1)} collective-permute-done((bf16[64,512]{1,0:T(8,128)(2,1)S(1)}, bf16[64,512]{1,0:T(8,128)(2,1)S(1)}, u32[]{:S(2)}, u32[]{:S(2)}) %collective-permute-start.5) | collective-permute-done | bytes 65568 | tf_op jit(solution)/shard_map/ppermute | solution.py:98
  22.2 1.3 %collective-permute-done.6 = bf16[64,512]{1,0:T(8,128)(2,1)S(1)} collective-permute-done((bf16[64,512]{1,0:T(8,128)(2,1)S(1)}, bf16[64,512]{1,0:T(8,128)(2,1)S(1)}, u32[]{:S(2)}, u32[]{:S(2)}) %collective-permute-start.6) | collective-permute-done | bytes 65568 | tf_op jit(solution)/shard_map/ppermute | solution.py:98
  23.5 2.4 %collective-permute-done.7 = bf16[64,512]{1,0:T(8,128)(2,1)S(1)} collective-permute-done((bf16[64,512]{1,0:T(8,128)(2,1)S(1)}, bf16[64,512]{1,0:T(8,128)(2,1)S(1)}, u32[]{:S(2)}, u32[]{:S(2)}) %collective-permute-start.7) | collective-permute-done | bytes 65568 | tf_op jit(solution)/shard_map/ppermute | solution.py:98
  25.9 0.7 %convert_add_fusion = f32[64,512]{1,0:T(8,128)} fusion(bf16[64,512]{1,0:T(8,128)(2,1)S(1)} %collective-permute-done.7, bf16[64,512]{1,0:T(8,128)(2,1)S(1)} %collective-permute-done.6, f32[64,512]{1,0:T(8,128)S(1)} %get-tuple-element.13, bf16[64,512]{1,0:T(8,128)(2,1)S(1)} %collective-permute-done.5), kind=kLoop, calls=%fused_computation | loop fusion | flops 196608 | bytes 458752 | tf_op jit(solution)/shard_map/add | solution.py:142
  (17 shorter events, 0.0 us)
Async XLA Ops:
  0.0 6.7 %collective-permute-start = (bf16[64,512]{1,0:T(8,128)(2,1)}, bf16[64,512]{1,0:T(8,128)(2,1)S(1)}, u32[]{:S(2)}, u32[]{:S(2)}) collective-permute-start(bf16[64,512]{1,0:T(8,128)(2,1)} %refs_0_.1), channel_id=1, source_target_pairs={{0,1},{1,0},{2,3},{3,2},{4,5},{5,4},{6,7},{7,6},{8,9},{9,8},{10,11... | collective-permute-start | bytes 196616 | tf_op jit(solution)/shard_map/ppermute | solution.py:98
  0.5 9.7 %collective-permute-start.1 = (bf16[64,512]{1,0:T(8,128)(2,1)}, bf16[64,512]{1,0:T(8,128)(2,1)S(1)}, u32[]{:S(2)}, u32[]{:S(2)}) collective-permute-start(bf16[64,512]{1,0:T(8,128)(2,1)} %refs_0_.1), channel_id=1, source_target_pairs={{0,6},{1,7},{2,4},{3,5},{4,2},{5,3},{6,0},{7,1},{8,14},{9,15},{10,... | collective-permute-start | bytes 196616 | tf_op jit(solution)/shard_map/ppermute | solution.py:98
  5.1 6.3 %collective-permute-start.3 = (bf16[64,512]{1,0:T(8,128)(2,1)}, bf16[64,512]{1,0:T(8,128)(2,1)S(1)}, u32[]{:S(2)}, u32[]{:S(2)}) collective-permute-start(bf16[64,512]{1,0:T(8,128)(2,1)} %refs_0_.1), channel_id=1, source_target_pairs={{0,4},{1,5},{2,6},{3,7},{4,0},{5,1},{6,2},{7,3},{8,12},{9,13},{10,... | collective-permute-start | bytes 196616 | tf_op jit(solution)/shard_map/ppermute | solution.py:98
  5.1 5.2 %collective-permute-start.2 = (bf16[64,512]{1,0:T(8,128)(2,1)}, bf16[64,512]{1,0:T(8,128)(2,1)S(1)}, u32[]{:S(2)}, u32[]{:S(2)}) collective-permute-start(bf16[64,512]{1,0:T(8,128)(2,1)} %refs_0_.1), channel_id=1, source_target_pairs={{0,2},{1,3},{2,0},{3,1},{4,6},{5,7},{6,4},{7,5},{8,10},{9,11},{10,... | collective-permute-start | bytes 196616 | tf_op jit(solution)/shard_map/ppermute | solution.py:98
  5.7 0.8 %copy-start.5 = (s32[16,8]{0,1:T(8,128)S(1)}, s32[16,8]{0,1:T(8,128)}, u32[]{:S(2)}) copy-start(s32[16,8]{0,1:T(8,128)} %param.12) | copy-start | bytes 1540
  5.7 0.7 %copy-start.6 = (s32[1,1,2,8]{3,2,1,0:T(2,128)S(1)}, s32[1,1,2,8]{3,2,1,0:T(2,128)}, u32[]{:S(2)}) copy-start(s32[1,1,2,8]{3,2,1,0:T(2,128)} %param.14) | copy-start | bytes 196
  6.5 0.7 %copy-start.3 = (s32[1,4096]{1,0:T(1,128)S(1)}, s32[1,4096]{1,0:T(1,128)}, u32[]{:S(2)}) copy-start(s32[1,4096]{1,0:T(1,128)} %param.9) | copy-start | bytes 49156
  7.2 0.8 %copy-start.4 = (bf16[64,512]{1,0:T(8,128)(2,1)S(1)}, bf16[64,512]{1,0:T(8,128)(2,1)}, u32[]{:S(2)}) copy-start(bf16[64,512]{1,0:T(8,128)(2,1)} %refs_0_.1) | copy-start | bytes 196612
  10.2 2.8 %copy-start.2 = (bf16[1,1,8,256,256]{4,3,2,1,0:T(8,128)(2,1)S(1)}, bf16[1,1,8,256,256]{4,3,2,1,0:T(8,128)(2,1)}, u32[]{:S(2)}) copy-start(bf16[1,1,8,256,256]{4,3,2,1,0:T(8,128)(2,1)} %param.13) | copy-start | bytes 3145732
  11.4 1.7 %collective-permute-start.4 = (bf16[192,512]{1,0:T(8,128)(2,1)S(1)}, bf16[192,512]{1,0:T(8,128)(2,1)S(1)}, u32[]{:S(2)}, u32[]{:S(2)}) collective-permute-start(bf16[192,512]{1,0:T(8,128)(2,1)S(1)} %constant_dynamic-update-slice_fusion.refs_0_), channel_id=1, source_target_pairs={{0,1},{1,0},{2,3},{3,2},{4,5},{5,4},{6,7},{7,6},{8,9},{9,8},{10,11... | collective-permute-start | bytes 589832 | tf_op jit(solution)/shard_map/ppermute | solution.py:98
  11.4 1.7 %copy-start = (bf16[16,8,16,256]{3,2,1,0:T(8,128)(2,1)S(1)}, bf16[16,8,16,256]{3,2,1,0:T(8,128)(2,1)}, u32[]{:S(2)}) copy-start(bf16[16,8,16,256]{3,2,1,0:T(8,128)(2,1)} %left_ref.1) | copy-start | bytes 3145732
  11.4 1.7 %copy-start.1 = (bf16[16,8,16,256]{3,2,1,0:T(8,128)(2,1)S(1)}, bf16[16,8,16,256]{3,2,1,0:T(8,128)(2,1)}, u32[]{:S(2)}) copy-start(bf16[16,8,16,256]{3,2,1,0:T(8,128)(2,1)} %right_ref.1) | copy-start | bytes 3145732
  17.6 4.5 %collective-permute-start.5 = (bf16[64,512]{1,0:T(8,128)(2,1)S(1)}, bf16[64,512]{1,0:T(8,128)(2,1)S(1)}, u32[]{:S(2)}, u32[]{:S(2)}) collective-permute-start(bf16[64,512]{1,0:T(8,128)(2,1)S(1)} %get-tuple-element.14), channel_id=1, source_target_pairs={{0,8},{8,0},{16,24},{24,16},{1,9},{9,1},{17,25},{25,17},{2,10},{10... | collective-permute-start | bytes 196616 | tf_op jit(solution)/shard_map/ppermute | solution.py:98
  19.2 4.3 %collective-permute-start.6 = (bf16[64,512]{1,0:T(8,128)(2,1)S(1)}, bf16[64,512]{1,0:T(8,128)(2,1)S(1)}, u32[]{:S(2)}, u32[]{:S(2)}) collective-permute-start(bf16[64,512]{1,0:T(8,128)(2,1)S(1)} %get-tuple-element.15), channel_id=1, source_target_pairs={{0,16},{8,24},{16,0},{24,8},{1,17},{9,25},{17,1},{25,9},{2,18},{10... | collective-permute-start | bytes 196616 | tf_op jit(solution)/shard_map/ppermute | solution.py:98
  20.7 5.2 %collective-permute-start.7 = (bf16[64,512]{1,0:T(8,128)(2,1)S(1)}, bf16[64,512]{1,0:T(8,128)(2,1)S(1)}, u32[]{:S(2)}, u32[]{:S(2)}) collective-permute-start(bf16[64,512]{1,0:T(8,128)(2,1)S(1)} %get-tuple-element.16), channel_id=1, source_target_pairs={{0,24},{8,16},{16,8},{24,0},{1,25},{9,17},{17,9},{25,1},{2,26},{10... | collective-permute-start | bytes 196616 | tf_op jit(solution)/shard_map/ppermute | solution.py:98

commit v3 on v2

--- a/solution.py
+++ b/solution.py
@@ -12,6 +12,7 @@
 VMEM = pl.BlockSpec(memory_space=pltpu.VMEM)
 SMEM = pl.BlockSpec(memory_space=pltpu.SMEM)
 ROW, COL, COUNT, INDEX = 0, 1, 2, 3
+CODE_BITS = 14.97
 
 
 def slab_blocks(meta_ref, slabs, width):
@@ -30,6 +31,9 @@
     low = jnp.bitwise_and(order, width - 1)
     high = jnp.right_shift(order, width.bit_length() - 1)
     onehot = jnp.where(lax.broadcasted_iota(jnp.int32, (width, width), 0) == low, 1.0, 0.0).astype(BF16)
+    if blocks[0][0].shape[0] == rows:
+        stacked = jnp.concatenate([ref[:, half * width : (half + 1) * width] for ref, half, _ in blocks], 0)
+        blocks = [(stacked, 0, sum([ids for _, _, ids in blocks], []))]
     for ref, half, ids in blocks:
         picked = jnp.dot(ref[:, half * width : (half + 1) * width], onehot, preferred_element_type=F32)
         for slot, own in enumerate(ids):
@@ -59,8 +63,9 @@
     blocks = slab_blocks(meta_ref, slabs, width)
     lane = lax.broadcasted_iota(jnp.int32, (1, lanes), 1)
     for tile in range(tiles):
-        x = reorder_tile(tile, order_ref, blocks, part_ref[tile].astype(F32)).astype(BF16)
-        x_ref[tile] = x
+        x_ref[tile] = reorder_tile(tile, order_ref, blocks, part_ref[tile].astype(F32)).astype(BF16)
+    for tile in range(tiles):
+        x = x_ref[tile]
         left = left_ref[tile].reshape(lanes, width)
         projected = lax.dot_general(x, left, (((1,), (1,)), ((), ())), preferred_element_type=F32)
         for col in range(cols):
@@ -86,8 +91,24 @@
         out_ref[:, part * 128 : (part + 1) * 128] = sum_ref[row * parts + part]
     for distance, send_ref in enumerate(send_refs, 1):
         to = jnp.bitwise_xor(row, distance)
-        for part in range(parts):
-            send_ref[:, part * 128 : (part + 1) * 128] = sum_ref[to * parts + part].astype(send_ref.dtype)
+        block = sum_ref[pl.ds(to * parts, parts)].reshape(parts * rows, 128)
+        most = jnp.max(jnp.abs(block), axis=(0, 1), keepdims=True)
+        power = jnp.ceil(jnp.log2(jnp.maximum(most, 1e-30)) - CODE_BITS)
+        code = jnp.clip(jnp.round(block * jnp.exp2(-power)), -32767.0, 32767.0)
+        send_ref[: parts * rows] = code.astype(jnp.int32).astype(jnp.int16)
+        send_ref[parts * rows :] = jnp.broadcast_to(power.astype(jnp.int32), (16, 128)).astype(jnp.int16)
+
+
+def finish_kernel(own_ref, *refs):
+    *got_refs, out_ref = refs
+    rows = own_ref.shape[0]
+    parts = own_ref.shape[1] // 128
+    steps = [jnp.exp2(got_ref[parts * rows :].astype(F32)[:1]) for got_ref in got_refs]
+    for part in range(parts):
+        total = own_ref[:, part * 128 : (part + 1) * 128]
+        for got_ref, step in zip(got_refs, steps):
+            total = total + got_ref[part * rows : (part + 1) * rows].astype(F32) * step
+        out_ref[:, part * 128 : (part + 1) * 128] = total
 
 
 def local(sizes, adjoint, panel_order, left, right, tile_ranks, near_blocks, near_index, near_count):
@@ -113,7 +134,7 @@
         )(meta, order, *slabs, *([] if part is None else [part]))
 
     if own_cols % width == 0:
-        far_off = [n_col - 2] + list(range(2, n_col - 2, 2))
+        far_off = [6, 4, 2]
         beside = swap(adjoint, "col", n_col, 1)
         near_part, got = reorder([adjoint, beside], [[0], [1]], spare=len(far_off) * rows)
         for at, d in enumerate(far_off):
@@ -127,7 +148,7 @@
     out, *sends = pl.pallas_call(
         functools.partial(main_kernel, last_off),
         out_shape=[jax.ShapeDtypeStruct((rows, out_cols), F32)]
-        + [jax.ShapeDtypeStruct((rows, out_cols), BF16)] * (n_row - 1),
+        + [jax.ShapeDtypeStruct((rows * out_cols // 128 + 16, 128), jnp.int16)] * (n_row - 1),
         in_specs=[SMEM] + [VMEM] * (5 + len(last)),
         out_specs=[VMEM] * n_row,
         scratch_shapes=[
@@ -138,9 +159,15 @@
         compiler_params=pltpu.CompilerParams(vmem_limit_bytes=32 << 20),
         name="apply",
     )(meta, order, left, right, near_blocks[0, 0], part, *last)
-    for distance, send in enumerate(sends, 1):
-        out = out + swap(send, "row", n_row, distance).astype(F32)
-    return out
+    got = [swap(sends[d - 1], "row", n_row, d) for d in range(n_row - 1, 0, -1)]
+    return pl.pallas_call(
+        finish_kernel,
+        out_shape=jax.ShapeDtypeStruct((rows, out_cols), F32),
+        in_specs=[VMEM] * n_row,
+        out_specs=VMEM,
+        compiler_params=pltpu.CompilerParams(vmem_limit_bytes=4 << 20),
+        name="finish",
+    )(out, *got)
 
 
 def solution(mesh):

time: 26.8 us -> 24.4 us (0.910)
  Pallas kernels: 8.27 us -> 6.97 us
  other arithmetic: 0.68 us -> 0 us
  waiting for transfers between devices: 5.89 us -> 5.35 us
    pallas_call x1, Pallas kernels: 4.5 us -> 3.12 us  [local(): pl.pallas_call(functools.partial(main_kernel, last_off), out_shape=[jax.S...]
    pallas_call x0 -> x1, Pallas kernels: none -> 0.71 us  [local(): pl.pallas_call(finish_kernel, out_shape=jax.ShapeDtypeStruct((rows, out_c...]
    add x1 -> x0, other arithmetic: 0.68 us -> none  [local(): out = out + swap(send, 'row', n_row, distance).astype(F32)]
    pallas_call x2, Pallas kernels: 3.76 us -> 3.14 us  [reorder(): pl.pallas_call(functools.partial(reorder_kernel, distances, part is None)...]
    ppermute x8, waiting for transfers between devices: 5.89 us -> 5.35 us  [local(): lax.ppermute(x, axis, [(i, i ^ d) for i in range(n)])]
  transfers between devices with their start and end apart: 8 -> 8, of which waited for: 5 -> 4; matrix products, arithmetic and copies ran while one was open for 1% -> 1% of each run, Pallas kernels for 14% -> 13%
where the time goes in v3:
time: 24.4 us; the launch traced here: 24.2 us
  starting transfers between devices  9.31 us (38%)
  Pallas kernels  6.97 us (29%)
  waiting for transfers between devices  5.35 us (22%)
  local copies, waits for them, and re-layouts  1.76 us (7%)
  between operations  0.8 us (3%)
    ppermute x8, starting transfers between devices, local(): lax.ppermute(x, axis, [(i, i ^ d) for i in range(n)])  9.31 us
    ppermute x8, waiting for transfers between devices, local(): lax.ppermute(x, axis, [(i, i ^ d) for i in range(n)])  5.35 us
    pallas_call x2, Pallas kernels, reorder(): pl.pallas_call(functools.partial(reorder_kernel, distances, part is None)...  3.14 us
    pallas_call x1, Pallas kernels, local(): pl.pallas_call(functools.partial(main_kernel, last_off), out_shape=[jax.S...  3.12 us
    unnamed x15, local copies, waits for them, and re-layouts  1.49 us
    pallas_call x1, Pallas kernels, local(): pl.pallas_call(finish_kernel, out_shape=jax.ShapeDtypeStruct((rows, out_c...  0.71 us
  transfers between devices with their start and end apart: 8, of which 4 were waited for; matrix products, arithmetic and copies ran while one was open for 1% of the time, Pallas kernels for 13%

profile of v3, /device:TPU:0, one launch (start us, length us, event | category | flops | bytes accessed | tf_op | source)
XLA Modules:
  0.0 24.2 jit_solution(6179065644504252819)
XLA Ops:
  0.0 0.5 %collective-permute-start = (bf16[64,512]{1,0:T(8,128)(2,1)}, bf16[64,512]{1,0:T(8,128)(2,1)S(1)}, u32[]{:S(2)}, u32[]{:S(2)}) collective-permute-start(bf16[64,512]{1,0:T(8,128)(2,1)} %refs_0_.1), channel_id=1, source_target_pairs={{0,1},{1,0},{2,3},{3,2},{4,5},{5,4},{6,7},{7,6},{8,9},{9,8},{10,11... | collective-permute-start | bytes 196616 | tf_op jit(solution)/shard_map/ppermute | solution.py:119
  0.5 4.6 %collective-permute-start.1 = (bf16[64,512]{1,0:T(8,128)(2,1)}, bf16[64,512]{1,0:T(8,128)(2,1)S(1)}, u32[]{:S(2)}, u32[]{:S(2)}) collective-permute-start(bf16[64,512]{1,0:T(8,128)(2,1)} %refs_0_.1), channel_id=1, source_target_pairs={{0,6},{1,7},{2,4},{3,5},{4,2},{5,3},{6,0},{7,1},{8,14},{9,15},{10,... | collective-permute-start | bytes 196616 | tf_op jit(solution)/shard_map/ppermute | solution.py:119
  5.1 0.6 %collective-permute-start.2 = (bf16[64,512]{1,0:T(8,128)(2,1)}, bf16[64,512]{1,0:T(8,128)(2,1)S(1)}, u32[]{:S(2)}, u32[]{:S(2)}) collective-permute-start(bf16[64,512]{1,0:T(8,128)(2,1)} %refs_0_.1), channel_id=1, source_target_pairs={{0,4},{1,5},{2,6},{3,7},{4,0},{5,1},{6,2},{7,3},{8,12},{9,13},{10,... | collective-permute-start | bytes 196616 | tf_op jit(solution)/shard_map/ppermute | solution.py:119
  6.4 0.0 copy-done.6
  6.4 0.1 reshape.9
  6.5 0.1 copy.10
  6.5 0.1 reshape.10
  6.6 0.1 concatenate.3.meta_ref
  6.7 0.5 %copy-done.3 = s32[1,4096]{1,0:T(1,128)S(1)} copy-done((s32[1,4096]{1,0:T(1,128)S(1)}, s32[1,4096]{1,0:T(1,128)}, u32[]{:S(2)}) %copy-start.3) | copy-done | bytes 16408
  7.2 0.8 %copy-done.4 = bf16[64,512]{1,0:T(8,128)(2,1)S(1)} copy-done((bf16[64,512]{1,0:T(8,128)(2,1)S(1)}, bf16[64,512]{1,0:T(8,128)(2,1)}, u32[]{:S(2)}) %copy-start.4) | copy-done | bytes 65560
  8.0 1.5 %reorder.2 = (bf16[16,64,256]{2,1,0:T(8,128)(2,1)S(1)}, bf16[192,512]{1,0:T(8,128)(2,1)S(1)}) custom-call(s32[147]{0:T(256)S(1)} %concatenate.3.meta_ref, s32[16,1,256]{2,1,0:T(1,128)S(1)} %bitcast.7, bf16[64,512]{1,0:T(8,128)(2,1)S(1)} %copy-done.4, bf16[64,512]{1,0:T(8,128)(2,1)S(1)} %collective-permute-done.refs_1_), custom_call_target="tpu_custom_call" | custom-call | flops 536870912 | tf_op jit(solution)/shard_map/reorder/pallas_call | solution.py:125
  9.6 1.6 %collective-permute-done.2 = bf16[64,512]{1,0:T(8,128)(2,1)S(1)} collective-permute-done((bf16[64,512]{1,0:T(8,128)(2,1)}, bf16[64,512]{1,0:T(8,128)(2,1)S(1)}, u32[]{:S(2)}, u32[]{:S(2)}) %collective-permute-start.2) | collective-permute-done | bytes 65568 | tf_op jit(solution)/shard_map/ppermute | solution.py:119
  11.2 0.1 collective-permute-start.4
  11.3 0.0 copy-start
  11.3 1.6 %reorder.3.part_ref = bf16[16,64,256]{2,1,0:T(8,128)(2,1)S(1)} custom-call(s32[147]{0:T(256)S(1)} %concatenate.3.meta_ref, s32[16,1,256]{2,1,0:T(1,128)S(1)} %bitcast.8, bf16[192,512]{1,0:T(8,128)(2,1)S(1)} %constant_dynamic-update-slice_fusion.refs_0_, bf16[16,64,256]{2,1,0:T(8,128)(2,1)S(1)} %get-tuple-element.12.refs_1_), custom_call_target="tpu_custom_call" | custom-call | flops 805306368 | tf_op jit(solution)/shard_map/reorder/pallas_call | solution.py:125
  13.0 0.1 copy-done.1
  13.0 3.1 %apply.1 = (f32[64,512]{1,0:T(8,128)S(1)}, s16[272,128]{1,0:T(8,128)(2,1)S(1)}, s16[272,128]{1,0:T(8,128)(2,1)S(1)}, s16[272,128]{1,0:T(8,128)(2,1)S(1)}) custom-call(s32[147]{0:T(256)S(1)} %concatenate.3.meta_ref, s32[16,1,256]{2,1,0:T(1,128)S(1)} %bitcast.9, bf16[16,8,16,256]{3,2,1,0:T(8,128)(2,1)S(1)} %copy-done, bf16[16,8,16,256]{3,2,1,0:T(8,128)(2,1)S(1)} %copy-done.1, ...), custom_call_target="tpu_custom_call" | custom-call | tf_op jit(solution)/shard_map/apply/pallas_call | solution.py:148
  16.2 2.5 %collective-permute-start.5 = (s16[272,128]{1,0:T(8,128)(2,1)S(1)}, s16[272,128]{1,0:T(8,128)(2,1)S(1)}, u32[]{:S(2)}, u32[]{:S(2)}) collective-permute-start(s16[272,128]{1,0:T(8,128)(2,1)S(1)} %get-tuple-element.14), channel_id=1, source_target_pairs={{0,24},{8,16},{16,8},{24,0},{1,25},{9,17},{17,9},{25,1},{2,26},{10... | collective-permute-start | bytes 208904 | tf_op jit(solution)/shard_map/ppermute | solution.py:119
  18.7 0.5 %collective-permute-start.6 = (s16[272,128]{1,0:T(8,128)(2,1)S(1)}, s16[272,128]{1,0:T(8,128)(2,1)S(1)}, u32[]{:S(2)}, u32[]{:S(2)}) collective-permute-start(s16[272,128]{1,0:T(8,128)(2,1)S(1)} %get-tuple-element.15), channel_id=1, source_target_pairs={{0,16},{8,24},{16,0},{24,8},{1,17},{9,25},{17,1},{25,9},{2,18},{10... | collective-permute-start | bytes 208904 | tf_op jit(solution)/shard_map/ppermute | solution.py:119
  19.2 0.5 %collective-permute-start.7 = (s16[272,128]{1,0:T(8,128)(2,1)S(1)}, s16[272,128]{1,0:T(8,128)(2,1)S(1)}, u32[]{:S(2)}, u32[]{:S(2)}) collective-permute-start(s16[272,128]{1,0:T(8,128)(2,1)S(1)} %get-tuple-element.16), channel_id=1, source_target_pairs={{0,8},{8,0},{16,24},{24,16},{1,9},{9,1},{17,25},{25,17},{2,10},{10... | collective-permute-start | bytes 208904 | tf_op jit(solution)/shard_map/ppermute | solution.py:119
  19.7 1.9 %collective-permute-done.5.refs_0_ = s16[272,128]{1,0:T(8,128)(2,1)S(1)} collective-permute-done((s16[272,128]{1,0:T(8,128)(2,1)S(1)}, s16[272,128]{1,0:T(8,128)(2,1)S(1)}, u32[]{:S(2)}, u32[]{:S(2)}) %collective-permute-start.5) | collective-permute-done | bytes 69664 | tf_op jit(solution)/shard_map/ppermute | solution.py:119
  21.7 1.5 %collective-permute-done.6.refs_1_ = s16[272,128]{1,0:T(8,128)(2,1)S(1)} collective-permute-done((s16[272,128]{1,0:T(8,128)(2,1)S(1)}, s16[272,128]{1,0:T(8,128)(2,1)S(1)}, u32[]{:S(2)}, u32[]{:S(2)}) %collective-permute-start.6) | collective-permute-done | bytes 69664 | tf_op jit(solution)/shard_map/ppermute | solution.py:119
  23.1 0.4 %collective-permute-done.7.refs_2_ = s16[272,128]{1,0:T(8,128)(2,1)S(1)} collective-permute-done((s16[272,128]{1,0:T(8,128)(2,1)S(1)}, s16[272,128]{1,0:T(8,128)(2,1)S(1)}, u32[]{:S(2)}, u32[]{:S(2)}) %collective-permute-start.7) | collective-permute-done | bytes 69664 | tf_op jit(solution)/shard_map/ppermute | solution.py:119
  23.5 0.7 %finish.1 = f32[64,512]{1,0:T(8,128)} custom-call(f32[64,512]{1,0:T(8,128)S(1)} %get-tuple-element.13.own_ref, s16[272,128]{1,0:T(8,128)(2,1)S(1)} %collective-permute-done.5.refs_0_, s16[272,128]{1,0:T(8,128)(2,1)S(1)} %collective-permute-done.6.refs_1_, s16[272,128]{1,0:T(8,128)(2,1)S(1)} %collective-permute-done.7.refs_2_), custom_call_target="tpu_custom_call" | custom-call | tf_op jit(solution)/shard_map/finish/pallas_call | solution.py:163
  (17 shorter events, 0.1 us)
Async XLA Ops:
  0.0 6.7 %collective-permute-start = (bf16[64,512]{1,0:T(8,128)(2,1)}, bf16[64,512]{1,0:T(8,128)(2,1)S(1)}, u32[]{:S(2)}, u32[]{:S(2)}) collective-permute-start(bf16[64,512]{1,0:T(8,128)(2,1)} %refs_0_.1), channel_id=1, source_target_pairs={{0,1},{1,0},{2,3},{3,2},{4,5},{5,4},{6,7},{7,6},{8,9},{9,8},{10,11... | collective-permute-start | bytes 196616 | tf_op jit(solution)/shard_map/ppermute | solution.py:119
  0.5 9.1 %collective-permute-start.1 = (bf16[64,512]{1,0:T(8,128)(2,1)}, bf16[64,512]{1,0:T(8,128)(2,1)S(1)}, u32[]{:S(2)}, u32[]{:S(2)}) collective-permute-start(bf16[64,512]{1,0:T(8,128)(2,1)} %refs_0_.1), channel_id=1, source_target_pairs={{0,6},{1,7},{2,4},{3,5},{4,2},{5,3},{6,0},{7,1},{8,14},{9,15},{10,... | collective-permute-start | bytes 196616 | tf_op jit(solution)/shard_map/ppermute | solution.py:119
  5.1 6.1 %collective-permute-start.3 = (bf16[64,512]{1,0:T(8,128)(2,1)}, bf16[64,512]{1,0:T(8,128)(2,1)S(1)}, u32[]{:S(2)}, u32[]{:S(2)}) collective-permute-start(bf16[64,512]{1,0:T(8,128)(2,1)} %refs_0_.1), channel_id=1, source_target_pairs={{0,2},{1,3},{2,0},{3,1},{4,6},{5,7},{6,4},{7,5},{8,10},{9,11},{10,... | collective-permute-start | bytes 196616 | tf_op jit(solution)/shard_map/ppermute | solution.py:119
  5.1 6.1 %collective-permute-start.2 = (bf16[64,512]{1,0:T(8,128)(2,1)}, bf16[64,512]{1,0:T(8,128)(2,1)S(1)}, u32[]{:S(2)}, u32[]{:S(2)}) collective-permute-start(bf16[64,512]{1,0:T(8,128)(2,1)} %refs_0_.1), channel_id=1, source_target_pairs={{0,4},{1,5},{2,6},{3,7},{4,0},{5,1},{6,2},{7,3},{8,12},{9,13},{10,... | collective-permute-start | bytes 196616 | tf_op jit(solution)/shard_map/ppermute | solution.py:119
  5.7 0.8 %copy-start.5 = (s32[16,8]{0,1:T(8,128)S(1)}, s32[16,8]{0,1:T(8,128)}, u32[]{:S(2)}) copy-start(s32[16,8]{0,1:T(8,128)} %param.12) | copy-start | bytes 1540
  5.7 0.7 %copy-start.6 = (s32[1,1,2,8]{3,2,1,0:T(2,128)S(1)}, s32[1,1,2,8]{3,2,1,0:T(2,128)}, u32[]{:S(2)}) copy-start(s32[1,1,2,8]{3,2,1,0:T(2,128)} %param.14) | copy-start | bytes 196
  6.5 0.7 %copy-start.3 = (s32[1,4096]{1,0:T(1,128)S(1)}, s32[1,4096]{1,0:T(1,128)}, u32[]{:S(2)}) copy-start(s32[1,4096]{1,0:T(1,128)} %param.9) | copy-start | bytes 49156
  7.2 0.8 %copy-start.4 = (bf16[64,512]{1,0:T(8,128)(2,1)S(1)}, bf16[64,512]{1,0:T(8,128)(2,1)}, u32[]{:S(2)}) copy-start(bf16[64,512]{1,0:T(8,128)(2,1)} %refs_0_.1) | copy-start | bytes 196612
  11.1 1.8 %copy-start.2 = (bf16[1,1,8,256,256]{4,3,2,1,0:T(8,128)(2,1)S(1)}, bf16[1,1,8,256,256]{4,3,2,1,0:T(8,128)(2,1)}, u32[]{:S(2)}) copy-start(bf16[1,1,8,256,256]{4,3,2,1,0:T(8,128)(2,1)} %param.13) | copy-start | bytes 3145732
  11.2 1.7 %collective-permute-start.4 = (bf16[192,512]{1,0:T(8,128)(2,1)S(1)}, bf16[192,512]{1,0:T(8,128)(2,1)S(1)}, u32[]{:S(2)}, u32[]{:S(2)}) collective-permute-start(bf16[192,512]{1,0:T(8,128)(2,1)S(1)} %constant_dynamic-update-slice_fusion.refs_0_), channel_id=1, source_target_pairs={{0,1},{1,0},{2,3},{3,2},{4,5},{5,4},{6,7},{7,6},{8,9},{9,8},{10,11... | collective-permute-start | bytes 589832 | tf_op jit(solution)/shard_map/ppermute | solution.py:119
  11.3 1.7 %copy-start = (bf16[16,8,16,256]{3,2,1,0:T(8,128)(2,1)S(1)}, bf16[16,8,16,256]{3,2,1,0:T(8,128)(2,1)}, u32[]{:S(2)}) copy-start(bf16[16,8,16,256]{3,2,1,0:T(8,128)(2,1)} %left_ref.1) | copy-start | bytes 3145732
  11.3 1.8 %copy-start.1 = (bf16[16,8,16,256]{3,2,1,0:T(8,128)(2,1)S(1)}, bf16[16,8,16,256]{3,2,1,0:T(8,128)(2,1)}, u32[]{:S(2)}) copy-start(bf16[16,8,16,256]{3,2,1,0:T(8,128)(2,1)} %right_ref.1) | copy-start | bytes 3145732
  16.2 5.5 %collective-permute-start.5 = (s16[272,128]{1,0:T(8,128)(2,1)S(1)}, s16[272,128]{1,0:T(8,128)(2,1)S(1)}, u32[]{:S(2)}, u32[]{:S(2)}) collective-permute-start(s16[272,128]{1,0:T(8,128)(2,1)S(1)} %get-tuple-element.14), channel_id=1, source_target_pairs={{0,24},{8,16},{16,8},{24,0},{1,25},{9,17},{17,9},{25,1},{2,26},{10... | collective-permute-start | bytes 208904 | tf_op jit(solution)/shard_map/ppermute | solution.py:119
  18.7 4.5 %collective-permute-start.6 = (s16[272,128]{1,0:T(8,128)(2,1)S(1)}, s16[272,128]{1,0:T(8,128)(2,1)S(1)}, u32[]{:S(2)}, u32[]{:S(2)}) collective-permute-start(s16[272,128]{1,0:T(8,128)(2,1)S(1)} %get-tuple-element.15), channel_id=1, source_target_pairs={{0,16},{8,24},{16,0},{24,8},{1,17},{9,25},{17,1},{25,9},{2,18},{10... | collective-permute-start | bytes 208904 | tf_op jit(solution)/shard_map/ppermute | solution.py:119
  19.2 4.3 %collective-permute-start.7 = (s16[272,128]{1,0:T(8,128)(2,1)S(1)}, s16[272,128]{1,0:T(8,128)(2,1)S(1)}, u32[]{:S(2)}, u32[]{:S(2)}) collective-permute-start(s16[272,128]{1,0:T(8,128)(2,1)S(1)} %get-tuple-element.16), channel_id=1, source_target_pairs={{0,8},{8,0},{16,24},{24,16},{1,9},{9,1},{17,25},{25,17},{2,10},{10... | collective-permute-start | bytes 208904 | tf_op jit(solution)/shard_map/ppermute | solution.py:119

commit v4 on v3

--- a/solution.py
+++ b/solution.py
@@ -10,18 +10,16 @@
 F32 = jnp.float32
 BF16 = jnp.bfloat16
 VMEM = pl.BlockSpec(memory_space=pltpu.VMEM)
-SMEM = pl.BlockSpec(memory_space=pltpu.SMEM)
-ROW, COL, COUNT, INDEX = 0, 1, 2, 3
+ANY = pl.BlockSpec(memory_space=pl.ANY)
+ROW, COUNT, INDEX = 0, 1, 2
 CODE_BITS = 14.97
 
 
-def slab_blocks(meta_ref, slabs, width):
+def slab_blocks(slabs, width):
     blocks = []
     for ref, distances in slabs:
         halves = ref.shape[1] // width
-        for half in range(halves):
-            ids = [half if d is None else jnp.bitwise_xor(meta_ref[COL], d) * halves + half for d in distances]
-            blocks.append((ref, half, ids))
+        blocks += [(ref, half, [distance * halves + half for distance in distances]) for half in range(halves)]
     return blocks
 
 
@@ -41,29 +39,32 @@
     return total
 
 
-def reorder_kernel(distances, first, meta_ref, order_ref, *refs):
-    out_ref = refs[len(distances) + (not first)]
-    for spare_ref in refs[len(distances) + (not first) + 1 :]:
+def reorder_kernel(distances, first, order_ref, *refs):
+    out_ref = refs[len(distances) + 1]
+    for spare_ref in refs[len(distances) + 2 :]:
         spare_ref[...] = jnp.zeros(spare_ref.shape, spare_ref.dtype)
     slabs = list(zip(refs, distances))
     tiles, rows, width = out_ref.shape
-    blocks = slab_blocks(meta_ref, slabs, width)
+    blocks = slab_blocks(slabs, width)
     for tile in range(tiles):
         total = jnp.zeros((rows, width), F32) if first else refs[len(distances)][tile].astype(F32)
         out_ref[tile] = reorder_tile(tile, order_ref, blocks, total).astype(BF16)
 
 
-def main_kernel(distances, meta_ref, order_ref, left_ref, right_ref, near_ref, part_ref, *refs):
+def main_kernel(distances, meta_hbm, order_ref, left_ref, right_ref, near_ref, part_ref, *refs):
     slabs = list(zip(refs, distances))
-    out_ref, *send_refs, x_ref, wide_ref, sum_ref = refs[len(distances) :]
+    out_ref, *send_refs, x_ref, wide_ref, sum_ref, meta_ref, meta_sem = refs[len(distances) :]
+    meta_copy = pltpu.make_async_copy(meta_hbm, meta_ref, meta_sem)
+    meta_copy.start()
     tiles, rows, width = x_ref.shape
     _, cols, rank_most, _ = left_ref.shape
     slot_most = near_ref.shape[0]
     lanes = cols * rank_most
-    blocks = slab_blocks(meta_ref, slabs, width)
+    blocks = slab_blocks(slabs, width)
     lane = lax.broadcasted_iota(jnp.int32, (1, lanes), 1)
     for tile in range(tiles):
         x_ref[tile] = reorder_tile(tile, order_ref, blocks, part_ref[tile].astype(F32)).astype(BF16)
+    meta_copy.wait()
     for tile in range(tiles):
         x = x_ref[tile]
         left = left_ref[tile].reshape(lanes, width)
@@ -115,10 +116,10 @@
     n_row, n_col = sizes
     rows, own_cols = adjoint.shape
     tiles, cols, rank_most, width = left.shape
-    order = panel_order.reshape(tiles, 1, width)
     swap = lambda x, axis, n, d: lax.ppermute(x, axis, [(i, i ^ d) for i in range(n)])
-    place = jnp.stack([lax.axis_index("row"), lax.axis_index("col"), near_count[0, 0]]).astype(jnp.int32)
+    place = jnp.stack([lax.axis_index("row"), near_count[0, 0]]).astype(jnp.int32)
     meta = jnp.concatenate([place, near_index.reshape(-1), tile_ranks.reshape(-1)])
+    meta = jnp.pad(meta, (0, -meta.shape[0] % 128))
 
     def reorder(slabs, distances, part=None, spare=0):
         slots = sum(slab.shape[0] * slab.shape[1] for slab in slabs)
@@ -126,15 +127,16 @@
             functools.partial(reorder_kernel, distances, part is None),
             out_shape=[jax.ShapeDtypeStruct((tiles, rows, width), BF16)]
             + ([jax.ShapeDtypeStruct((spare, own_cols), BF16)] if spare else []),
-            in_specs=[SMEM] + [VMEM] * (1 + len(slabs) + (part is not None)),
+            in_specs=[VMEM] * (1 + len(slabs) + (part is not None)) + [ANY] * (part is None),
             out_specs=[VMEM] * (1 + (spare > 0)),
-            cost_estimate=pl.CostEstimate(flops=2 * slots * tiles * width, bytes_accessed=0, transcendentals=0),
+            cost_estimate=pl.CostEstimate(flops=2 * slots * tiles * width if part is None else 1000, bytes_accessed=0, transcendentals=0),
             compiler_params=pltpu.CompilerParams(vmem_limit_bytes=16 << 20),
             name="reorder",
-        )(meta, order, *slabs, *([] if part is None else [part]))
+        )(order, *slabs, meta if part is None else part)
 
-    if own_cols % width == 0:
-        far_off = [6, 4, 2]
+    if own_cols % width == 0 and own_cols & (own_cols - 1) == 0:
+        order = jnp.bitwise_xor(panel_order, lax.axis_index("col") * own_cols).reshape(tiles, 1, width)
+        far_off = [n_col - 2] + list(range(2, n_col - 2, 2))
         beside = swap(adjoint, "col", n_col, 1)
         near_part, got = reorder([adjoint, beside], [[0], [1]], spare=len(far_off) * rows)
         for at, d in enumerate(far_off):
@@ -142,19 +144,22 @@
         last, last_off = [swap(got, "col", n_col, 1)], [[d ^ 1 for d in far_off]]
         (part,) = reorder([got], [far_off], near_part)
     else:
+        order = panel_order.reshape(tiles, 1, width)
         part = jnp.zeros((tiles, rows, width), BF16)
-        last, last_off = [lax.all_gather(adjoint, "col", axis=1, tiled=True)], [[None]]
+        last, last_off = [lax.all_gather(adjoint, "col", axis=1, tiled=True)], [[0]]
     out_cols = cols * width // n_row
     out, *sends = pl.pallas_call(
         functools.partial(main_kernel, last_off),
         out_shape=[jax.ShapeDtypeStruct((rows, out_cols), F32)]
         + [jax.ShapeDtypeStruct((rows * out_cols // 128 + 16, 128), jnp.int16)] * (n_row - 1),
-        in_specs=[SMEM] + [VMEM] * (5 + len(last)),
+        in_specs=[ANY] + [VMEM] * (5 + len(last)),
         out_specs=[VMEM] * n_row,
         scratch_shapes=[
             pltpu.VMEM((tiles, rows, width), BF16),
             pltpu.VMEM((tiles, cols * rows, cols * rank_most), BF16),
             pltpu.VMEM((cols * width // 128, rows, 128), F32),
+            pltpu.SMEM(meta.shape, jnp.int32),
+            pltpu.SemaphoreType.DMA(()),
         ],
         compiler_params=pltpu.CompilerParams(vmem_limit_bytes=32 << 20),
         name="apply",

time: 24.4 us -> 23.6 us (0.967)
  Pallas kernels: 6.97 us -> 5.34 us
  other arithmetic: 0 us -> 0.81 us
    pallas_call x2, Pallas kernels: 3.14 us -> 2.04 us  [reorder(): pl.pallas_call(functools.partial(reorder_kernel, distances, part is None)...]
    xor x0 -> x1, other arithmetic: none -> 0.73 us  [local(): jnp.bitwise_xor(panel_order, lax.axis_index('col') * own_cols)]
    unnamed x15 -> x9, local copies, waits for them, and re-layouts: 1.49 us -> 0.78 us
    reshape x1, local copies, waits for them, and re-layouts: 0.08 us -> 0.76 us  [local(): near_index.reshape(-1)]
    pallas_call x1, Pallas kernels: 3.12 us -> 2.6 us  [local(): pl.pallas_call(functools.partial(main_kernel, last_off), out_shape=[jax.S...]
  transfers between devices with their start and end apart: 8 -> 8, of which waited for: 4 -> 5; matrix products, arithmetic and copies ran while one was open for 1% -> 10% of each run, Pallas kernels for 13% -> 9%
where the time goes in v4:
time: 23.6 us; the launch traced here: 23.4 us
  starting transfers between devices  9.38 us (40%)
  waiting for transfers between devices  5.42 us (23%)
  Pallas kernels  5.34 us (23%)
  local copies, waits for them, and re-layouts  1.65 us (7%)
  other arithmetic  0.81 us (3%)
  between operations  0.77 us (3%)
    ppermute x8, starting transfers between devices, local(): lax.ppermute(x, axis, [(i, i ^ d) for i in range(n)])  9.38 us
    ppermute x8, waiting for transfers between devices, local(): lax.ppermute(x, axis, [(i, i ^ d) for i in range(n)])  5.42 us
    pallas_call x1, Pallas kernels, local(): pl.pallas_call(functools.partial(main_kernel, last_off), out_shape=[jax.S...  2.6 us
    pallas_call x2, Pallas kernels, reorder(): pl.pallas_call(functools.partial(reorder_kernel, distances, part is None)...  2.04 us
    unnamed x9, local copies, waits for them, and re-layouts  0.78 us
    reshape x1, local copies, waits for them, and re-layouts, local(): near_index.reshape(-1)  0.76 us
    xor x1, other arithmetic, local(): jnp.bitwise_xor(panel_order, lax.axis_index('col') * own_cols)  0.73 us
    pallas_call x1, Pallas kernels, local(): pl.pallas_call(finish_kernel, out_shape=jax.ShapeDtypeStruct((rows, out_c...  0.71 us
  transfers between devices with their start and end apart: 8, of which 5 were waited for; matrix products, arithmetic and copies ran while one was open for 10% of the time, Pallas kernels for 9%

profile of v4, /device:TPU:0, one launch (start us, length us, event | category | flops | bytes accessed | tf_op | source)
XLA Modules:
  0.0 23.4 jit_solution(3625998756765046170)
XLA Ops:
  0.0 5.0 %collective-permute-start.1 = (bf16[64,512]{1,0:T(8,128)(2,1)}, bf16[64,512]{1,0:T(8,128)(2,1)S(1)}, u32[]{:S(2)}, u32[]{:S(2)}) collective-permute-start(bf16[64,512]{1,0:T(8,128)(2,1)} %refs_0_.1), channel_id=1, source_target_pairs={{0,6},{1,7},{2,4},{3,5},{4,2},{5,3},{6,0},{7,1},{8,14},{9,15},{10,... | collective-permute-start | bytes 196616 | tf_op jit(solution)/shard_map/ppermute | solution.py:119
  5.1 0.0 collective-permute-start
  5.1 0.7 %collective-permute-start.2 = (bf16[64,512]{1,0:T(8,128)(2,1)}, bf16[64,512]{1,0:T(8,128)(2,1)S(1)}, u32[]{:S(2)}, u32[]{:S(2)}) collective-permute-start(bf16[64,512]{1,0:T(8,128)(2,1)} %refs_0_.1), channel_id=1, source_target_pairs={{0,2},{1,3},{2,0},{3,1},{4,6},{5,7},{6,4},{7,5},{8,10},{9,11},{10,... | collective-permute-start | bytes 196616 | tf_op jit(solution)/shard_map/ppermute | solution.py:119
  6.4 0.8 %reshape.9 = s32[16]{0:T(128)S(1)} reshape(s32[1,1,2,8]{3,2,1,0:T(2,128)} %param.14) | data formatting | bytes 128 | tf_op jit(solution)/shard_map/reshape | solution.py:121
  7.2 0.8 %copy.10 = s32[16,8]{1,0:T(8,128)S(1)} copy(s32[16,8]{0,1:T(8,128)} %param.12) | data formatting | bytes 1024 | tf_op args[4]
  7.9 0.1 reshape.10
  8.0 0.7 %broadcast_xor_fusion = s32[1,4096]{1,0:T(1,128)S(1)} fusion(s32[1,4096]{1,0:T(1,128)} %param.9, s32[]{:T(128)S(6)} %mul.3), kind=kLoop, calls=%fused_computation | loop fusion | flops 4096 | bytes 32772 | tf_op jit(solution)/shard_map/xor | solution.py:138
  8.8 0.1 pad_add_fusion
  8.9 0.0 copy-start.1
  8.9 0.0 copy-start.2
  8.9 1.0 %reorder.2 = (bf16[16,64,256]{2,1,0:T(8,128)(2,1)S(1)}, bf16[192,512]{1,0:T(8,128)(2,1)S(1)}) custom-call(s32[16,1,256]{2,1,0:T(1,128)S(1)} %bitcast.6, bf16[64,512]{1,0:T(8,128)(2,1)S(1)} %copy-done.3, bf16[64,512]{1,0:T(8,128)(2,1)S(1)} %collective-permute-done.refs_1_, s32[256]{0:T(256)S(1)} %pad.4.refs_2_.meta_hbm), custom_call_target="tpu_custom_call" | custom-call | flops 536870912 | tf_op jit(solution)/shard_map/reorder/pallas_call | solution.py:126
  9.9 0.0 copy-start
  9.9 1.3 %collective-permute-done.2 = bf16[64,512]{1,0:T(8,128)(2,1)S(1)} collective-permute-done((bf16[64,512]{1,0:T(8,128)(2,1)}, bf16[64,512]{1,0:T(8,128)(2,1)S(1)}, u32[]{:S(2)}, u32[]{:S(2)}) %collective-permute-start.2) | collective-permute-done | bytes 65568 | tf_op jit(solution)/shard_map/ppermute | solution.py:119
  11.2 0.1 collective-permute-start.4
  11.3 1.1 %reorder.3.part_ref = bf16[16,64,256]{2,1,0:T(8,128)(2,1)S(1)} custom-call(s32[16,1,256]{2,1,0:T(1,128)S(1)} %bitcast.7, bf16[192,512]{1,0:T(8,128)(2,1)S(1)} %constant_dynamic-update-slice_fusion.refs_0_, bf16[16,64,256]{2,1,0:T(8,128)(2,1)S(1)} %get-tuple-element.12.refs_1_), custom_call_target="tpu_custom_call" | custom-call | flops 1000 | tf_op jit(solution)/shard_map/reorder/pallas_call | solution.py:126
  12.4 0.4 %collective-permute-done.4.refs_0_ = bf16[192,512]{1,0:T(8,128)(2,1)S(1)} collective-permute-done((bf16[192,512]{1,0:T(8,128)(2,1)S(1)}, bf16[192,512]{1,0:T(8,128)(2,1)S(1)}, u32[]{:S(2)}, u32[]{:S(2)}) %collective-permute-start.4) | collective-permute-done | bytes 196640 | tf_op jit(solution)/shard_map/ppermute | solution.py:119
  12.7 2.6 %apply.1 = (f32[64,512]{1,0:T(8,128)S(1)}, s16[272,128]{1,0:T(8,128)(2,1)S(1)}, s16[272,128]{1,0:T(8,128)(2,1)S(1)}, s16[272,128]{1,0:T(8,128)(2,1)S(1)}) custom-call(s32[256]{0:T(256)S(1)} %pad.4.refs_2_.meta_hbm, s32[16,1,256]{2,1,0:T(1,128)S(1)} %bitcast.8, bf16[16,8,16,256]{3,2,1,0:T(8,128)(2,1)S(1)} %copy-done, bf16[16,8,16,256]{3,2,1,0:T(8,128)(2,1)S(1)} %copy-done.1, ...), custom_call_target="tpu_custom_call" | custom-call | tf_op jit(solution)/shard_map/apply/pallas_call | solution.py:151
  15.3 2.5 %collective-permute-start.5 = (s16[272,128]{1,0:T(8,128)(2,1)S(1)}, s16[272,128]{1,0:T(8,128)(2,1)S(1)}, u32[]{:S(2)}, u32[]{:S(2)}) collective-permute-start(s16[272,128]{1,0:T(8,128)(2,1)S(1)} %get-tuple-element.14), channel_id=1, source_target_pairs={{0,24},{8,16},{16,8},{24,0},{1,25},{9,17},{17,9},{25,1},{2,26},{10... | collective-permute-start | bytes 208904 | tf_op jit(solution)/shard_map/ppermute | solution.py:119
  17.8 0.5 %collective-permute-start.6 = (s16[272,128]{1,0:T(8,128)(2,1)S(1)}, s16[272,128]{1,0:T(8,128)(2,1)S(1)}, u32[]{:S(2)}, u32[]{:S(2)}) collective-permute-start(s16[272,128]{1,0:T(8,128)(2,1)S(1)} %get-tuple-element.15), channel_id=1, source_target_pairs={{0,16},{8,24},{16,0},{24,8},{1,17},{9,25},{17,1},{25,9},{2,18},{10... | collective-permute-start | bytes 208904 | tf_op jit(solution)/shard_map/ppermute | solution.py:119
  18.4 0.5 %collective-permute-start.7 = (s16[272,128]{1,0:T(8,128)(2,1)S(1)}, s16[272,128]{1,0:T(8,128)(2,1)S(1)}, u32[]{:S(2)}, u32[]{:S(2)}) collective-permute-start(s16[272,128]{1,0:T(8,128)(2,1)S(1)} %get-tuple-element.16), channel_id=1, source_target_pairs={{0,8},{8,0},{16,24},{24,16},{1,9},{9,1},{17,25},{25,17},{2,10},{10... | collective-permute-start | bytes 208904 | tf_op jit(solution)/shard_map/ppermute | solution.py:119
  18.9 1.7 %collective-permute-done.5.refs_0_ = s16[272,128]{1,0:T(8,128)(2,1)S(1)} collective-permute-done((s16[272,128]{1,0:T(8,128)(2,1)S(1)}, s16[272,128]{1,0:T(8,128)(2,1)S(1)}, u32[]{:S(2)}, u32[]{:S(2)}) %collective-permute-start.5) | collective-permute-done | bytes 69664 | tf_op jit(solution)/shard_map/ppermute | solution.py:119
  20.6 1.5 %collective-permute-done.6.refs_1_ = s16[272,128]{1,0:T(8,128)(2,1)S(1)} collective-permute-done((s16[272,128]{1,0:T(8,128)(2,1)S(1)}, s16[272,128]{1,0:T(8,128)(2,1)S(1)}, u32[]{:S(2)}, u32[]{:S(2)}) %collective-permute-start.6) | collective-permute-done | bytes 69664 | tf_op jit(solution)/shard_map/ppermute | solution.py:119
  22.1 0.5 %collective-permute-done.7.refs_2_ = s16[272,128]{1,0:T(8,128)(2,1)S(1)} collective-permute-done((s16[272,128]{1,0:T(8,128)(2,1)S(1)}, s16[272,128]{1,0:T(8,128)(2,1)S(1)}, u32[]{:S(2)}, u32[]{:S(2)}) %collective-permute-start.7) | collective-permute-done | bytes 69664 | tf_op jit(solution)/shard_map/ppermute | solution.py:119
  22.7 0.7 %finish.1 = f32[64,512]{1,0:T(8,128)} custom-call(f32[64,512]{1,0:T(8,128)S(1)} %get-tuple-element.13.own_ref, s16[272,128]{1,0:T(8,128)(2,1)S(1)} %collective-permute-done.5.refs_0_, s16[272,128]{1,0:T(8,128)(2,1)S(1)} %collective-permute-done.6.refs_1_, s16[272,128]{1,0:T(8,128)(2,1)S(1)} %collective-permute-done.7.refs_2_), custom_call_target="tpu_custom_call" | custom-call | tf_op jit(solution)/shard_map/finish/pallas_call | solution.py:168
  (13 shorter events, 0.0 us)
Async XLA Ops:
  0.0 8.8 %copy-start.3 = (bf16[64,512]{1,0:T(8,128)(2,1)S(1)}, bf16[64,512]{1,0:T(8,128)(2,1)}, u32[]{:S(2)}) copy-start(bf16[64,512]{1,0:T(8,128)(2,1)} %refs_0_.1) | copy-start | bytes 196612
  0.0 9.9 %collective-permute-start.1 = (bf16[64,512]{1,0:T(8,128)(2,1)}, bf16[64,512]{1,0:T(8,128)(2,1)S(1)}, u32[]{:S(2)}, u32[]{:S(2)}) collective-permute-start(bf16[64,512]{1,0:T(8,128)(2,1)} %refs_0_.1), channel_id=1, source_target_pairs={{0,6},{1,7},{2,4},{3,5},{4,2},{5,3},{6,0},{7,1},{8,14},{9,15},{10,... | collective-permute-start | bytes 196616 | tf_op jit(solution)/shard_map/ppermute | solution.py:119
  5.1 3.8 %collective-permute-start = (bf16[64,512]{1,0:T(8,128)(2,1)}, bf16[64,512]{1,0:T(8,128)(2,1)S(1)}, u32[]{:S(2)}, u32[]{:S(2)}) collective-permute-start(bf16[64,512]{1,0:T(8,128)(2,1)} %refs_0_.1), channel_id=1, source_target_pairs={{0,1},{1,0},{2,3},{3,2},{4,5},{5,4},{6,7},{7,6},{8,9},{9,8},{10,11... | collective-permute-start | bytes 196616 | tf_op jit(solution)/shard_map/ppermute | solution.py:119
  5.1 6.1 %collective-permute-start.3 = (bf16[64,512]{1,0:T(8,128)(2,1)}, bf16[64,512]{1,0:T(8,128)(2,1)S(1)}, u32[]{:S(2)}, u32[]{:S(2)}) collective-permute-start(bf16[64,512]{1,0:T(8,128)(2,1)} %refs_0_.1), channel_id=1, source_target_pairs={{0,4},{1,5},{2,6},{3,7},{4,0},{5,1},{6,2},{7,3},{8,12},{9,13},{10,... | collective-permute-start | bytes 196616 | tf_op jit(solution)/shard_map/ppermute | solution.py:119
  5.1 6.1 %collective-permute-start.2 = (bf16[64,512]{1,0:T(8,128)(2,1)}, bf16[64,512]{1,0:T(8,128)(2,1)S(1)}, u32[]{:S(2)}, u32[]{:S(2)}) collective-permute-start(bf16[64,512]{1,0:T(8,128)(2,1)} %refs_0_.1), channel_id=1, source_target_pairs={{0,2},{1,3},{2,0},{3,1},{4,6},{5,7},{6,4},{7,5},{8,10},{9,11},{10,... | collective-permute-start | bytes 196616 | tf_op jit(solution)/shard_map/ppermute | solution.py:119
  8.9 3.9 %copy-start.1 = (bf16[16,8,16,256]{3,2,1,0:T(8,128)(2,1)S(1)}, bf16[16,8,16,256]{3,2,1,0:T(8,128)(2,1)}, u32[]{:S(2)}) copy-start(bf16[16,8,16,256]{3,2,1,0:T(8,128)(2,1)} %right_ref.1) | copy-start | bytes 3145732
  8.9 3.9 %copy-start.2 = (bf16[1,1,8,256,256]{4,3,2,1,0:T(8,128)(2,1)S(1)}, bf16[1,1,8,256,256]{4,3,2,1,0:T(8,128)(2,1)}, u32[]{:S(2)}) copy-start(bf16[1,1,8,256,256]{4,3,2,1,0:T(8,128)(2,1)} %param.13) | copy-start | bytes 3145732
  9.9 2.9 %copy-start = (bf16[16,8,16,256]{3,2,1,0:T(8,128)(2,1)S(1)}, bf16[16,8,16,256]{3,2,1,0:T(8,128)(2,1)}, u32[]{:S(2)}) copy-start(bf16[16,8,16,256]{3,2,1,0:T(8,128)(2,1)} %left_ref.1) | copy-start | bytes 3145732
  11.2 1.5 %collective-permute-start.4 = (bf16[192,512]{1,0:T(8,128)(2,1)S(1)}, bf16[192,512]{1,0:T(8,128)(2,1)S(1)}, u32[]{:S(2)}, u32[]{:S(2)}) collective-permute-start(bf16[192,512]{1,0:T(8,128)(2,1)S(1)} %constant_dynamic-update-slice_fusion.refs_0_), channel_id=1, source_target_pairs={{0,1},{1,0},{2,3},{3,2},{4,5},{5,4},{6,7},{7,6},{8,9},{9,8},{10,11... | collective-permute-start | bytes 589832 | tf_op jit(solution)/shard_map/ppermute | solution.py:119
  15.3 5.3 %collective-permute-start.5 = (s16[272,128]{1,0:T(8,128)(2,1)S(1)}, s16[272,128]{1,0:T(8,128)(2,1)S(1)}, u32[]{:S(2)}, u32[]{:S(2)}) collective-permute-start(s16[272,128]{1,0:T(8,128)(2,1)S(1)} %get-tuple-element.14), channel_id=1, source_target_pairs={{0,24},{8,16},{16,8},{24,0},{1,25},{9,17},{17,9},{25,1},{2,26},{10... | collective-permute-start | bytes 208904 | tf_op jit(solution)/shard_map/ppermute | solution.py:119
  17.8 4.3 %collective-permute-start.6 = (s16[272,128]{1,0:T(8,128)(2,1)S(1)}, s16[272,128]{1,0:T(8,128)(2,1)S(1)}, u32[]{:S(2)}, u32[]{:S(2)}) collective-permute-start(s16[272,128]{1,0:T(8,128)(2,1)S(1)} %get-tuple-element.15), channel_id=1, source_target_pairs={{0,16},{8,24},{16,0},{24,8},{1,17},{9,25},{17,1},{25,9},{2,18},{10... | collective-permute-start | bytes 208904 | tf_op jit(solution)/shard_map/ppermute | solution.py:119
  18.4 4.3 %collective-permute-start.7 = (s16[272,128]{1,0:T(8,128)(2,1)S(1)}, s16[272,128]{1,0:T(8,128)(2,1)S(1)}, u32[]{:S(2)}, u32[]{:S(2)}) collective-permute-start(s16[272,128]{1,0:T(8,128)(2,1)S(1)} %get-tuple-element.16), channel_id=1, source_target_pairs={{0,8},{8,0},{16,24},{24,16},{1,9},{9,1},{17,25},{25,17},{2,10},{10... | collective-permute-start | bytes 208904 | tf_op jit(solution)/shard_map/ppermute | solution.py:119

commit v5 on v4

--- a/solution.py
+++ b/solution.py
@@ -11,7 +11,7 @@
 BF16 = jnp.bfloat16
 VMEM = pl.BlockSpec(memory_space=pltpu.VMEM)
 ANY = pl.BlockSpec(memory_space=pl.ANY)
-ROW, COUNT, INDEX = 0, 1, 2
+COUNT, INDEX = 0, 1
 CODE_BITS = 14.97
 
 
@@ -39,9 +39,27 @@
     return total
 
 
+def pack_scalars(small, small_refs, sems, packed_ref):
+    copies = [pltpu.make_async_copy(a, b, sems.at[at]) for at, (a, b) in enumerate(zip(small, small_refs))]
+    for copy in copies:
+        copy.start()
+    for copy in copies:
+        copy.wait()
+    at = 0
+    for ref in small_refs:
+        for i in range(ref.shape[0]):
+            for j in range(ref.shape[1]):
+                packed_ref[at] = ref[i, j]
+                at += 1
+
+
 def reorder_kernel(distances, first, order_ref, *refs):
-    out_ref = refs[len(distances) + 1]
-    for spare_ref in refs[len(distances) + 2 :]:
+    out_ref = refs[len(distances) + (3 if first else 1)]
+    if first:
+        *refs, s0, s1, s2, sems = refs
+        pack_scalars(refs[len(distances) : len(distances) + 3], (s0, s1, s2), sems, refs[-1])
+        refs = refs[:-1]
+    for spare_ref in refs[len(distances) + (3 if first else 1) + 1 :]:
         spare_ref[...] = jnp.zeros(spare_ref.shape, spare_ref.dtype)
     slabs = list(zip(refs, distances))
     tiles, rows, width = out_ref.shape
@@ -60,33 +78,32 @@
     _, cols, rank_most, _ = left_ref.shape
     slot_most = near_ref.shape[0]
     lanes = cols * rank_most
+    rank_at = lax.broadcasted_iota(jnp.int32, (rank_most, rows), 0)
     blocks = slab_blocks(slabs, width)
-    lane = lax.broadcasted_iota(jnp.int32, (1, lanes), 1)
     for tile in range(tiles):
         x_ref[tile] = reorder_tile(tile, order_ref, blocks, part_ref[tile].astype(F32)).astype(BF16)
     meta_copy.wait()
     for tile in range(tiles):
         x = x_ref[tile]
         left = left_ref[tile].reshape(lanes, width)
-        projected = lax.dot_general(x, left, (((1,), (1,)), ((), ())), preferred_element_type=F32)
+        projected = lax.dot_general(left, x, (((1,), (1,)), ((), ())), preferred_element_type=F32)
         for col in range(cols):
-            rank = meta_ref[INDEX + 2 * slot_most + tile * cols + col]
-            keep = (lane >= col * rank_most) & (lane < col * rank_most + rank)
-            wide_ref[tile, col * rows : (col + 1) * rows, :] = jnp.where(keep, projected, 0.0).astype(BF16)
-    wide = jnp.concatenate([wide_ref[tile] for tile in range(tiles)], axis=1)
-    right = right_ref[...].reshape(tiles * lanes, width)
-    far = jnp.dot(wide, right, preferred_element_type=F32)
+            keep = rank_at < meta_ref[INDEX + 2 * slot_most + col * tiles + tile]
+            kept = jnp.where(keep, projected[col * rank_most : (col + 1) * rank_most], 0.0)
+            wide_ref[col, tile * rank_most : (tile + 1) * rank_most, :] = kept.astype(BF16)
     pieces = width // 128
     for col in range(cols):
+        right = right_ref[:, col].reshape(tiles * rank_most, width)
+        far = lax.dot_general(wide_ref[col], right, (((0,), (0,)), ((), ())), preferred_element_type=F32)
         for piece in range(pieces):
-            sum_ref[col * pieces + piece] = far[col * rows : (col + 1) * rows, piece * 128 : (piece + 1) * 128]
+            sum_ref[col * pieces + piece] = far[:, piece * 128 : (piece + 1) * 128]
     for slot in range(slot_most):
         product = jnp.dot(x_ref[meta_ref[INDEX + slot]], near_ref[slot], preferred_element_type=F32)
         product = jnp.where(slot < meta_ref[COUNT], product, 0.0)
         at = meta_ref[INDEX + slot_most + slot] * pieces
         for piece in range(pieces):
             sum_ref[at + piece] += product[:, piece * 128 : (piece + 1) * 128]
-    row = meta_ref[ROW]
+    row = lax.axis_index("row")
     parts = out_ref.shape[1] // 128
     for part in range(parts):
         out_ref[:, part * 128 : (part + 1) * 128] = sum_ref[row * parts + part]
@@ -117,28 +134,28 @@
     rows, own_cols = adjoint.shape
     tiles, cols, rank_most, width = left.shape
     swap = lambda x, axis, n, d: lax.ppermute(x, axis, [(i, i ^ d) for i in range(n)])
-    place = jnp.stack([lax.axis_index("row"), near_count[0, 0]]).astype(jnp.int32)
-    meta = jnp.concatenate([place, near_index.reshape(-1), tile_ranks.reshape(-1)])
-    meta = jnp.pad(meta, (0, -meta.shape[0] % 128))
+    small = [near_count, near_index[0, 0], tile_ranks.T]
+    scalars = sum(x.size for x in small)
 
     def reorder(slabs, distances, part=None, spare=0):
         slots = sum(slab.shape[0] * slab.shape[1] for slab in slabs)
         return pl.pallas_call(
             functools.partial(reorder_kernel, distances, part is None),
             out_shape=[jax.ShapeDtypeStruct((tiles, rows, width), BF16)]
-            + ([jax.ShapeDtypeStruct((spare, own_cols), BF16)] if spare else []),
-            in_specs=[VMEM] * (1 + len(slabs) + (part is not None)) + [ANY] * (part is None),
-            out_specs=[VMEM] * (1 + (spare > 0)),
+            + ([jax.ShapeDtypeStruct((spare, own_cols), BF16), jax.ShapeDtypeStruct((-(-scalars // 128) * 128,), jnp.int32)] if spare else []),
+            in_specs=[VMEM] * (1 + len(slabs) + (part is not None)) + [ANY] * (3 if part is None else 0),
+            out_specs=[VMEM, VMEM, pl.BlockSpec(memory_space=pltpu.SMEM)] if spare else [VMEM],
+            scratch_shapes=[pltpu.SMEM(x.shape, jnp.int32) for x in small] + [pltpu.SemaphoreType.DMA((3,))] if spare else [],
             cost_estimate=pl.CostEstimate(flops=2 * slots * tiles * width if part is None else 1000, bytes_accessed=0, transcendentals=0),
             compiler_params=pltpu.CompilerParams(vmem_limit_bytes=16 << 20),
             name="reorder",
-        )(order, *slabs, meta if part is None else part)
+        )(order, *slabs, *(small if part is None else [part]))
 
     if own_cols % width == 0 and own_cols & (own_cols - 1) == 0:
         order = jnp.bitwise_xor(panel_order, lax.axis_index("col") * own_cols).reshape(tiles, 1, width)
         far_off = [n_col - 2] + list(range(2, n_col - 2, 2))
         beside = swap(adjoint, "col", n_col, 1)
-        near_part, got = reorder([adjoint, beside], [[0], [1]], spare=len(far_off) * rows)
+        near_part, got, meta = reorder([adjoint, beside], [[0], [1]], spare=len(far_off) * rows)
         for at, d in enumerate(far_off):
             got = lax.dynamic_update_slice_in_dim(got, swap(adjoint, "col", n_col, d), at * rows, 0)
         last, last_off = [swap(got, "col", n_col, 1)], [[d ^ 1 for d in far_off]]
@@ -146,6 +163,8 @@
     else:
         order = panel_order.reshape(tiles, 1, width)
         part = jnp.zeros((tiles, rows, width), BF16)
+        meta = jnp.concatenate([x.reshape(-1) for x in small])
+        meta = jnp.pad(meta, (0, -scalars % 128))
         last, last_off = [lax.all_gather(adjoint, "col", axis=1, tiled=True)], [[0]]
     out_cols = cols * width // n_row
     out, *sends = pl.pallas_call(
@@ -156,7 +175,7 @@
         out_specs=[VMEM] * n_row,
         scratch_shapes=[
             pltpu.VMEM((tiles, rows, width), BF16),
-            pltpu.VMEM((tiles, cols * rows, cols * rank_most), BF16),
+            pltpu.VMEM((cols, tiles * rank_most, rows), BF16),
             pltpu.VMEM((cols * width // 128, rows, 128), F32),
             pltpu.SMEM(meta.shape, jnp.int32),
             pltpu.SemaphoreType.DMA(()),

time: 23.6 us -> 23.2 us (0.983)
  waiting for transfers between devices: 5.42 us -> 4.5 us
  Pallas kernels: 5.34 us -> 6.06 us
    pallas_call x2, Pallas kernels: 2.04 us -> 3.21 us  [reorder(): pl.pallas_call(functools.partial(reorder_kernel, distances, part is None)...]
    ppermute x8, waiting for transfers between devices: 5.42 us -> 4.5 us  [local(): lax.ppermute(x, axis, [(i, i ^ d) for i in range(n)])]
    reshape x2 -> x0, local copies, waits for them, and re-layouts: 0.85 us -> none  [the longest x1 0.76 us: local(): near_index.reshape(-1)]
    unnamed x9 -> x12, local copies, waits for them, and re-layouts: 0.78 us -> 1.52 us
    pallas_call x1, Pallas kernels: 2.6 us -> 2.14 us  [local(): pl.pallas_call(functools.partial(main_kernel, last_off), out_shape=[jax.S...]
  transfers between devices with their start and end apart: 8 -> 8, of which waited for: 5 -> 5; matrix products, arithmetic and copies ran while one was open for 10% -> 3% of each run, Pallas kernels for 9% -> 14%
where the time goes in v5:
time: 23.2 us; the launch traced here: 22.9 us
  starting transfers between devices  9.31 us (40%)
  Pallas kernels  6.06 us (26%)
  waiting for transfers between devices  4.5 us (19%)
  local copies, waits for them, and re-layouts  1.54 us (7%)
  between operations  0.77 us (3%)
  other arithmetic  0.73 us (3%)
    ppermute x8, starting transfers between devices, local(): lax.ppermute(x, axis, [(i, i ^ d) for i in range(n)])  9.31 us
    ppermute x8, waiting for transfers between devices, local(): lax.ppermute(x, axis, [(i, i ^ d) for i in range(n)])  4.5 us
    pallas_call x2, Pallas kernels, reorder(): pl.pallas_call(functools.partial(reorder_kernel, distances, part is None)...  3.21 us
    pallas_call x1, Pallas kernels, local(): pl.pallas_call(functools.partial(main_kernel, last_off), out_shape=[jax.S...  2.14 us
    unnamed x12, local copies, waits for them, and re-layouts  1.52 us
    xor x1, other arithmetic, local(): jnp.bitwise_xor(panel_order, lax.axis_index('col') * own_cols)  0.73 us
    pallas_call x1, Pallas kernels, local(): pl.pallas_call(finish_kernel, out_shape=jax.ShapeDtypeStruct((rows, out_c...  0.71 us
  transfers between devices with their start and end apart: 8, of which 5 were waited for; matrix products, arithmetic and copies ran while one was open for 3% of the time, Pallas kernels for 14%

profile of v5, /device:TPU:0, one launch (start us, length us, event | category | flops | bytes accessed | tf_op | source)
XLA Modules:
  0.0 22.9 jit_solution(150499724450792797)
XLA Ops:
  0.0 5.0 %collective-permute-start.1 = (bf16[64,512]{1,0:T(8,128)(2,1)}, bf16[64,512]{1,0:T(8,128)(2,1)S(1)}, u32[]{:S(2)}, u32[]{:S(2)}) collective-permute-start(bf16[64,512]{1,0:T(8,128)(2,1)} %refs_0_.1), channel_id=1, source_target_pairs={{0,6},{1,7},{2,4},{3,5},{4,2},{5,3},{6,0},{7,1},{8,14},{9,15},{10,... | collective-permute-start | bytes 196616 | tf_op jit(solution)/shard_map/ppermute | solution.py:136
  5.0 0.0 collective-permute-start
  5.1 0.0 collective-permute-start.3
  5.1 0.6 %collective-permute-start.2 = (bf16[64,512]{1,0:T(8,128)(2,1)}, bf16[64,512]{1,0:T(8,128)(2,1)S(1)}, u32[]{:S(2)}, u32[]{:S(2)}) collective-permute-start(bf16[64,512]{1,0:T(8,128)(2,1)} %refs_0_.1), channel_id=1, source_target_pairs={{0,2},{1,3},{2,0},{3,1},{4,6},{5,7},{6,4},{7,5},{8,10},{9,11},{10,... | collective-permute-start | bytes 196616 | tf_op jit(solution)/shard_map/ppermute | solution.py:136
  5.7 0.7 %broadcast_xor_fusion = s32[1,4096]{1,0:T(1,128)S(1)} fusion(s32[1,4096]{1,0:T(1,128)} %param.9, s32[]{:T(128)S(6)} %mul.3), kind=kLoop, calls=%fused_computation | loop fusion | flops 4096 | bytes 32772 | tf_op jit(solution)/shard_map/xor | solution.py:155
  6.4 0.0 copy-start.4
  7.1 0.0 copy-start.5
  7.1 0.7 %copy-done.5 = s32[1,1,2,8]{3,2,1,0:T(2,128)S(1)} copy-done((s32[1,1,2,8]{3,2,1,0:T(2,128)S(1)}, s32[1,1,2,8]{3,2,1,0:T(2,128)}, u32[]{:S(2)}) %copy-start.5) | copy-done | bytes 88
  7.8 0.8 %copy-done.3 = bf16[64,512]{1,0:T(8,128)(2,1)S(1)} copy-done((bf16[64,512]{1,0:T(8,128)(2,1)S(1)}, bf16[64,512]{1,0:T(8,128)(2,1)}, u32[]{:S(2)}) %copy-start.3) | copy-done | bytes 65560
  8.6 2.2 %reorder.2 = (bf16[16,64,256]{2,1,0:T(8,128)(2,1)S(1)}, bf16[192,512]{1,0:T(8,128)(2,1)S(1)}, s32[256]{0:T(256)S(1)}) custom-call(s32[16,1,256]{2,1,0:T(1,128)S(1)} %bitcast.5, bf16[64,512]{1,0:T(8,128)(2,1)S(1)} %copy-done.3, bf16[64,512]{1,0:T(8,128)(2,1)S(1)} %collective-permute-done.refs_1_, s32[1,1]{1,0:T(1,128)S(6)} %copy.12.refs_2_, ...), custom_call_target="tpu_custom_call" | custom-call | flops 536870912 | tf_op jit(solution)/shard_map/reorder/pallas_call | solution.py:142
  10.8 0.0 copy-start
  10.8 0.0 collective-permute-done.1
  10.8 0.3 %collective-permute-done.2 = bf16[64,512]{1,0:T(8,128)(2,1)S(1)} collective-permute-done((bf16[64,512]{1,0:T(8,128)(2,1)}, bf16[64,512]{1,0:T(8,128)(2,1)S(1)}, u32[]{:S(2)}, u32[]{:S(2)}) %collective-permute-start.2) | collective-permute-done | bytes 65568 | tf_op jit(solution)/shard_map/ppermute | solution.py:136
  11.2 0.1 collective-permute-start.4
  11.3 1.0 %reorder.3.part_ref = bf16[16,64,256]{2,1,0:T(8,128)(2,1)S(1)} custom-call(s32[16,1,256]{2,1,0:T(1,128)S(1)} %bitcast.6, bf16[192,512]{1,0:T(8,128)(2,1)S(1)} %constant_dynamic-update-slice_fusion.refs_0_, bf16[16,64,256]{2,1,0:T(8,128)(2,1)S(1)} %get-tuple-element.14.refs_1_), custom_call_target="tpu_custom_call" | custom-call | flops 1000 | tf_op jit(solution)/shard_map/reorder/pallas_call | solution.py:142
  12.3 0.4 %collective-permute-done.4.refs_0_ = bf16[192,512]{1,0:T(8,128)(2,1)S(1)} collective-permute-done((bf16[192,512]{1,0:T(8,128)(2,1)S(1)}, bf16[192,512]{1,0:T(8,128)(2,1)S(1)}, u32[]{:S(2)}, u32[]{:S(2)}) %collective-permute-start.4) | collective-permute-done | bytes 196640 | tf_op jit(solution)/shard_map/ppermute | solution.py:136
  12.7 2.1 %apply.1 = (f32[64,512]{1,0:T(8,128)S(1)}, s16[272,128]{1,0:T(8,128)(2,1)S(1)}, s16[272,128]{1,0:T(8,128)(2,1)S(1)}, s16[272,128]{1,0:T(8,128)(2,1)S(1)}) custom-call(s32[256]{0:T(256)S(1)} %get-tuple-element.12.meta_hbm, s32[16,1,256]{2,1,0:T(1,128)S(1)} %bitcast.7, bf16[16,8,16,256]{3,2,1,0:T(8,128)(2,1)S(1)} %copy-done, ...), custom_call_target="tpu_custom_call" | custom-call | tf_op jit(solution)/shard_map/apply/pallas_call | solution.py:170
  14.9 2.5 %collective-permute-start.5 = (s16[272,128]{1,0:T(8,128)(2,1)S(1)}, s16[272,128]{1,0:T(8,128)(2,1)S(1)}, u32[]{:S(2)}, u32[]{:S(2)}) collective-permute-start(s16[272,128]{1,0:T(8,128)(2,1)S(1)} %get-tuple-element.16), channel_id=1, source_target_pairs={{0,24},{8,16},{16,8},{24,0},{1,25},{9,17},{17,9},{25,1},{2,26},{10... | collective-permute-start | bytes 208904 | tf_op jit(solution)/shard_map/ppermute | solution.py:136
  17.4 0.5 %collective-permute-start.6 = (s16[272,128]{1,0:T(8,128)(2,1)S(1)}, s16[272,128]{1,0:T(8,128)(2,1)S(1)}, u32[]{:S(2)}, u32[]{:S(2)}) collective-permute-start(s16[272,128]{1,0:T(8,128)(2,1)S(1)} %get-tuple-element.17), channel_id=1, source_target_pairs={{0,16},{8,24},{16,0},{24,8},{1,17},{9,25},{17,1},{25,9},{2,18},{10... | collective-permute-start | bytes 208904 | tf_op jit(solution)/shard_map/ppermute | solution.py:136
  17.9 0.5 %collective-permute-start.7 = (s16[272,128]{1,0:T(8,128)(2,1)S(1)}, s16[272,128]{1,0:T(8,128)(2,1)S(1)}, u32[]{:S(2)}, u32[]{:S(2)}) collective-permute-start(s16[272,128]{1,0:T(8,128)(2,1)S(1)} %get-tuple-element.18), channel_id=1, source_target_pairs={{0,8},{8,0},{16,24},{24,16},{1,9},{9,1},{17,25},{25,17},{2,10},{10... | collective-permute-start | bytes 208904 | tf_op jit(solution)/shard_map/ppermute | solution.py:136
  18.4 1.7 %collective-permute-done.5.refs_0_ = s16[272,128]{1,0:T(8,128)(2,1)S(1)} collective-permute-done((s16[272,128]{1,0:T(8,128)(2,1)S(1)}, s16[272,128]{1,0:T(8,128)(2,1)S(1)}, u32[]{:S(2)}, u32[]{:S(2)}) %collective-permute-start.5) | collective-permute-done | bytes 69664 | tf_op jit(solution)/shard_map/ppermute | solution.py:136
  20.2 1.5 %collective-permute-done.6.refs_1_ = s16[272,128]{1,0:T(8,128)(2,1)S(1)} collective-permute-done((s16[272,128]{1,0:T(8,128)(2,1)S(1)}, s16[272,128]{1,0:T(8,128)(2,1)S(1)}, u32[]{:S(2)}, u32[]{:S(2)}) %collective-permute-start.6) | collective-permute-done | bytes 69664 | tf_op jit(solution)/shard_map/ppermute | solution.py:136
  21.7 0.5 %collective-permute-done.7.refs_2_ = s16[272,128]{1,0:T(8,128)(2,1)S(1)} collective-permute-done((s16[272,128]{1,0:T(8,128)(2,1)S(1)}, s16[272,128]{1,0:T(8,128)(2,1)S(1)}, u32[]{:S(2)}, u32[]{:S(2)}) %collective-permute-start.7) | collective-permute-done | bytes 69664 | tf_op jit(solution)/shard_map/ppermute | solution.py:136
  22.2 0.7 %finish.1 = f32[64,512]{1,0:T(8,128)} custom-call(f32[64,512]{1,0:T(8,128)S(1)} %get-tuple-element.15.own_ref, s16[272,128]{1,0:T(8,128)(2,1)S(1)} %collective-permute-done.5.refs_0_, s16[272,128]{1,0:T(8,128)(2,1)S(1)} %collective-permute-done.6.refs_1_, s16[272,128]{1,0:T(8,128)(2,1)S(1)} %collective-permute-done.7.refs_2_), custom_call_target="tpu_custom_call" | custom-call | tf_op jit(solution)/shard_map/finish/pallas_call | solution.py:187
  (12 shorter events, 0.0 us)
Async XLA Ops:
  0.0 10.8 %collective-permute-start.1 = (bf16[64,512]{1,0:T(8,128)(2,1)}, bf16[64,512]{1,0:T(8,128)(2,1)S(1)}, u32[]{:S(2)}, u32[]{:S(2)}) collective-permute-start(bf16[64,512]{1,0:T(8,128)(2,1)} %refs_0_.1), channel_id=1, source_target_pairs={{0,6},{1,7},{2,4},{3,5},{4,2},{5,3},{6,0},{7,1},{8,14},{9,15},{10,... | collective-permute-start | bytes 196616 | tf_op jit(solution)/shard_map/ppermute | solution.py:136
  5.0 2.0 %collective-permute-start = (bf16[64,512]{1,0:T(8,128)(2,1)}, bf16[64,512]{1,0:T(8,128)(2,1)S(1)}, u32[]{:S(2)}, u32[]{:S(2)}) collective-permute-start(bf16[64,512]{1,0:T(8,128)(2,1)} %refs_0_.1), channel_id=1, source_target_pairs={{0,1},{1,0},{2,3},{3,2},{4,5},{5,4},{6,7},{7,6},{8,9},{9,8},{10,11... | collective-permute-start | bytes 196616 | tf_op jit(solution)/shard_map/ppermute | solution.py:136
  5.1 6.1 %collective-permute-start.3 = (bf16[64,512]{1,0:T(8,128)(2,1)}, bf16[64,512]{1,0:T(8,128)(2,1)S(1)}, u32[]{:S(2)}, u32[]{:S(2)}) collective-permute-start(bf16[64,512]{1,0:T(8,128)(2,1)} %refs_0_.1), channel_id=1, source_target_pairs={{0,4},{1,5},{2,6},{3,7},{4,0},{5,1},{6,2},{7,3},{8,12},{9,13},{10,... | collective-permute-start | bytes 196616 | tf_op jit(solution)/shard_map/ppermute | solution.py:136
  5.1 6.1 %collective-permute-start.2 = (bf16[64,512]{1,0:T(8,128)(2,1)}, bf16[64,512]{1,0:T(8,128)(2,1)S(1)}, u32[]{:S(2)}, u32[]{:S(2)}) collective-permute-start(bf16[64,512]{1,0:T(8,128)(2,1)} %refs_0_.1), channel_id=1, source_target_pairs={{0,2},{1,3},{2,0},{3,1},{4,6},{5,7},{6,4},{7,5},{8,10},{9,11},{10,... | collective-permute-start | bytes 196616 | tf_op jit(solution)/shard_map/ppermute | solution.py:136
  6.4 0.7 %copy-start.4 = (s32[16,8]{0,1:T(8,128)S(1)}, s32[16,8]{0,1:T(8,128)}, u32[]{:S(2)}) copy-start(s32[16,8]{0,1:T(8,128)} %param.12) | copy-start | bytes 1540
  7.1 0.7 %copy-start.5 = (s32[1,1,2,8]{3,2,1,0:T(2,128)S(1)}, s32[1,1,2,8]{3,2,1,0:T(2,128)}, u32[]{:S(2)}) copy-start(s32[1,1,2,8]{3,2,1,0:T(2,128)} %param.14) | copy-start | bytes 196
  7.8 0.8 %copy-start.3 = (bf16[64,512]{1,0:T(8,128)(2,1)S(1)}, bf16[64,512]{1,0:T(8,128)(2,1)}, u32[]{:S(2)}) copy-start(bf16[64,512]{1,0:T(8,128)(2,1)} %refs_0_.1) | copy-start | bytes 196612
  8.6 4.1 %copy-start.1 = (bf16[16,8,16,256]{3,2,1,0:T(8,128)(2,1)S(1)}, bf16[16,8,16,256]{3,2,1,0:T(8,128)(2,1)}, u32[]{:S(2)}) copy-start(bf16[16,8,16,256]{3,2,1,0:T(8,128)(2,1)} %right_ref.1) | copy-start | bytes 3145732
  8.6 4.1 %copy-start.2 = (bf16[1,1,8,256,256]{4,3,2,1,0:T(8,128)(2,1)S(1)}, bf16[1,1,8,256,256]{4,3,2,1,0:T(8,128)(2,1)}, u32[]{:S(2)}) copy-start(bf16[1,1,8,256,256]{4,3,2,1,0:T(8,128)(2,1)} %param.13) | copy-start | bytes 3145732
  10.8 1.9 %copy-start = (bf16[16,8,16,256]{3,2,1,0:T(8,128)(2,1)S(1)}, bf16[16,8,16,256]{3,2,1,0:T(8,128)(2,1)}, u32[]{:S(2)}) copy-start(bf16[16,8,16,256]{3,2,1,0:T(8,128)(2,1)} %left_ref.1) | copy-start | bytes 3145732
  11.2 1.5 %collective-permute-start.4 = (bf16[192,512]{1,0:T(8,128)(2,1)S(1)}, bf16[192,512]{1,0:T(8,128)(2,1)S(1)}, u32[]{:S(2)}, u32[]{:S(2)}) collective-permute-start(bf16[192,512]{1,0:T(8,128)(2,1)S(1)} %constant_dynamic-update-slice_fusion.refs_0_), channel_id=1, source_target_pairs={{0,1},{1,0},{2,3},{3,2},{4,5},{5,4},{6,7},{7,6},{8,9},{9,8},{10,11... | collective-permute-start | bytes 589832 | tf_op jit(solution)/shard_map/ppermute | solution.py:136
  14.9 5.3 %collective-permute-start.5 = (s16[272,128]{1,0:T(8,128)(2,1)S(1)}, s16[272,128]{1,0:T(8,128)(2,1)S(1)}, u32[]{:S(2)}, u32[]{:S(2)}) collective-permute-start(s16[272,128]{1,0:T(8,128)(2,1)S(1)} %get-tuple-element.16), channel_id=1, source_target_pairs={{0,24},{8,16},{16,8},{24,0},{1,25},{9,17},{17,9},{25,1},{2,26},{10... | collective-permute-start | bytes 208904 | tf_op jit(solution)/shard_map/ppermute | solution.py:136
  17.4 4.3 %collective-permute-start.6 = (s16[272,128]{1,0:T(8,128)(2,1)S(1)}, s16[272,128]{1,0:T(8,128)(2,1)S(1)}, u32[]{:S(2)}, u32[]{:S(2)}) collective-permute-start(s16[272,128]{1,0:T(8,128)(2,1)S(1)} %get-tuple-element.17), channel_id=1, source_target_pairs={{0,16},{8,24},{16,0},{24,8},{1,17},{9,25},{17,1},{25,9},{2,18},{10... | collective-permute-start | bytes 208904 | tf_op jit(solution)/shard_map/ppermute | solution.py:136
  17.9 4.3 %collective-permute-start.7 = (s16[272,128]{1,0:T(8,128)(2,1)S(1)}, s16[272,128]{1,0:T(8,128)(2,1)S(1)}, u32[]{:S(2)}, u32[]{:S(2)}) collective-permute-start(s16[272,128]{1,0:T(8,128)(2,1)S(1)} %get-tuple-element.18), channel_id=1, source_target_pairs={{0,8},{8,0},{16,24},{24,16},{1,9},{9,1},{17,25},{25,17},{2,10},{10... | collective-permute-start | bytes 208904 | tf_op jit(solution)/shard_map/ppermute | solution.py:136

commit v6 on v5

--- a/solution.py
+++ b/solution.py
@@ -67,6 +67,13 @@
     for tile in range(tiles):
         total = jnp.zeros((rows, width), F32) if first else refs[len(distances)][tile].astype(F32)
         out_ref[tile] = reorder_tile(tile, order_ref, blocks, total).astype(BF16)
+
+
+def row_step(row, distance, n_row):
+    if n_row != 4 or distance == 3:
+        return distance
+    turn = (row ^ (row >> 1)) & 1
+    return 1 + turn if distance == 1 else 2 - turn
 
 
 def main_kernel(distances, meta_hbm, order_ref, left_ref, right_ref, near_ref, part_ref, *refs):
@@ -108,7 +115,7 @@
     for part in range(parts):
         out_ref[:, part * 128 : (part + 1) * 128] = sum_ref[row * parts + part]
     for distance, send_ref in enumerate(send_refs, 1):
-        to = jnp.bitwise_xor(row, distance)
+        to = jnp.bitwise_xor(row, row_step(row, distance, len(send_refs) + 1))
         block = sum_ref[pl.ds(to * parts, parts)].reshape(parts * rows, 128)
         most = jnp.max(jnp.abs(block), axis=(0, 1), keepdims=True)
         power = jnp.ceil(jnp.log2(jnp.maximum(most, 1e-30)) - CODE_BITS)
@@ -183,7 +190,8 @@
         compiler_params=pltpu.CompilerParams(vmem_limit_bytes=32 << 20),
         name="apply",
     )(meta, order, left, right, near_blocks[0, 0], part, *last)
-    got = [swap(sends[d - 1], "row", n_row, d) for d in range(n_row - 1, 0, -1)]
+    steps = range(n_row - 1, 0, -1)
+    got = [lax.ppermute(sends[d - 1], "row", [(i, i ^ row_step(i, d, n_row)) for i in range(n_row)]) for d in steps]
     return pl.pallas_call(
         finish_kernel,
         out_shape=jax.ShapeDtypeStruct((rows, out_cols), F32),

time: 23.2 us -> 23.2 us (level)
  starting transfers between devices: 9.31 us -> 10.3 us
  waiting for transfers between devices: 4.5 us -> 3.51 us
    ppermute x0 -> x3, starting transfers between devices: none -> 4.54 us  [local(): lax.ppermute(sends[d - 1], 'row', [(i, i ^ row_step(i, d, n_row)) for i i...]
    ppermute x8 -> x5, waiting for transfers between devices: 4.5 us -> 0.72 us  [local(): lax.ppermute(x, axis, [(i, i ^ d) for i in range(n)])]
    ppermute x8 -> x5, starting transfers between devices: 9.31 us -> 5.76 us  [local(): lax.ppermute(x, axis, [(i, i ^ d) for i in range(n)])]
    ppermute x0 -> x3, waiting for transfers between devices: none -> 2.79 us  [local(): lax.ppermute(sends[d - 1], 'row', [(i, i ^ row_step(i, d, n_row)) for i i...]
where the time goes in v6:
time: 23.2 us; the launch traced here: 22.9 us
  starting transfers between devices  10.3 us (44%)
  Pallas kernels  6.06 us (26%)
  waiting for transfers between devices  3.51 us (15%)
  local copies, waits for them, and re-layouts  1.54 us (7%)
  between operations  0.77 us (3%)
  other arithmetic  0.73 us (3%)
    ppermute x5, starting transfers between devices, local(): lax.ppermute(x, axis, [(i, i ^ d) for i in range(n)])  5.76 us
    ppermute x3, starting transfers between devices, local(): lax.ppermute(sends[d - 1], 'row', [(i, i ^ row_step(i, d, n_row)) for i i...  4.54 us
    pallas_call x2, Pallas kernels, reorder(): pl.pallas_call(functools.partial(reorder_kernel, distances, part is None)...  3.21 us
    ppermute x3, waiting for transfers between devices, local(): lax.ppermute(sends[d - 1], 'row', [(i, i ^ row_step(i, d, n_row)) for i i...  2.79 us
    pallas_call x1, Pallas kernels, local(): pl.pallas_call(functools.partial(main_kernel, last_off), out_shape=[jax.S...  2.14 us
    unnamed x12, local copies, waits for them, and re-layouts  1.52 us
    xor x1, other arithmetic, local(): jnp.bitwise_xor(panel_order, lax.axis_index('col') * own_cols)  0.73 us
    ppermute x5, waiting for transfers between devices, local(): lax.ppermute(x, axis, [(i, i ^ d) for i in range(n)])  0.72 us
  transfers between devices with their start and end apart: 8, of which 5 were waited for; matrix products, arithmetic and copies ran while one was open for 3% of the time, Pallas kernels for 14%

profile of v6, /device:TPU:0, one launch (start us, length us, event | category | flops | bytes accessed | tf_op | source)
XLA Modules:
  0.0 22.9 jit_solution(580228184890257310)
XLA Ops:
  0.0 5.0 %collective-permute-start.1 = (bf16[64,512]{1,0:T(8,128)(2,1)}, bf16[64,512]{1,0:T(8,128)(2,1)S(1)}, u32[]{:S(2)}, u32[]{:S(2)}) collective-permute-start(bf16[64,512]{1,0:T(8,128)(2,1)} %refs_0_.1), channel_id=1, source_target_pairs={{0,6},{1,7},{2,4},{3,5},{4,2},{5,3},{6,0},{7,1},{8,14},{9,15},{10,... | collective-permute-start | bytes 196616 | tf_op jit(solution)/shard_map/ppermute | solution.py:143
  5.0 0.0 collective-permute-start
  5.1 0.0 collective-permute-start.3
  5.1 0.6 %collective-permute-start.2 = (bf16[64,512]{1,0:T(8,128)(2,1)}, bf16[64,512]{1,0:T(8,128)(2,1)S(1)}, u32[]{:S(2)}, u32[]{:S(2)}) collective-permute-start(bf16[64,512]{1,0:T(8,128)(2,1)} %refs_0_.1), channel_id=1, source_target_pairs={{0,2},{1,3},{2,0},{3,1},{4,6},{5,7},{6,4},{7,5},{8,10},{9,11},{10,... | collective-permute-start | bytes 196616 | tf_op jit(solution)/shard_map/ppermute | solution.py:143
  5.7 0.7 %broadcast_xor_fusion = s32[1,4096]{1,0:T(1,128)S(1)} fusion(s32[1,4096]{1,0:T(1,128)} %param.9, s32[]{:T(128)S(6)} %mul.3), kind=kLoop, calls=%fused_computation | loop fusion | flops 4096 | bytes 32772 | tf_op jit(solution)/shard_map/xor | solution.py:162
  6.4 0.0 copy-start.4
  7.1 0.0 copy-start.5
  7.1 0.7 %copy-done.5 = s32[1,1,2,8]{3,2,1,0:T(2,128)S(1)} copy-done((s32[1,1,2,8]{3,2,1,0:T(2,128)S(1)}, s32[1,1,2,8]{3,2,1,0:T(2,128)}, u32[]{:S(2)}) %copy-start.5) | copy-done | bytes 88
  7.8 0.8 %copy-done.3 = bf16[64,512]{1,0:T(8,128)(2,1)S(1)} copy-done((bf16[64,512]{1,0:T(8,128)(2,1)S(1)}, bf16[64,512]{1,0:T(8,128)(2,1)}, u32[]{:S(2)}) %copy-start.3) | copy-done | bytes 65560
  8.6 2.2 %reorder.2 = (bf16[16,64,256]{2,1,0:T(8,128)(2,1)S(1)}, bf16[192,512]{1,0:T(8,128)(2,1)S(1)}, s32[256]{0:T(256)S(1)}) custom-call(s32[16,1,256]{2,1,0:T(1,128)S(1)} %bitcast.5, bf16[64,512]{1,0:T(8,128)(2,1)S(1)} %copy-done.3, bf16[64,512]{1,0:T(8,128)(2,1)S(1)} %collective-permute-done.refs_1_, s32[1,1]{1,0:T(1,128)S(6)} %copy.12.refs_2_, ...), custom_call_target="tpu_custom_call" | custom-call | flops 536870912 | tf_op jit(solution)/shard_map/reorder/pallas_call | solution.py:149
  10.8 0.0 copy-start
  10.8 0.0 collective-permute-done.1
  10.8 0.3 %collective-permute-done.2 = bf16[64,512]{1,0:T(8,128)(2,1)S(1)} collective-permute-done((bf16[64,512]{1,0:T(8,128)(2,1)}, bf16[64,512]{1,0:T(8,128)(2,1)S(1)}, u32[]{:S(2)}, u32[]{:S(2)}) %collective-permute-start.2) | collective-permute-done | bytes 65568 | tf_op jit(solution)/shard_map/ppermute | solution.py:143
  11.2 0.1 collective-permute-start.4
  11.3 1.0 %reorder.3.part_ref = bf16[16,64,256]{2,1,0:T(8,128)(2,1)S(1)} custom-call(s32[16,1,256]{2,1,0:T(1,128)S(1)} %bitcast.6, bf16[192,512]{1,0:T(8,128)(2,1)S(1)} %constant_dynamic-update-slice_fusion.refs_0_, bf16[16,64,256]{2,1,0:T(8,128)(2,1)S(1)} %get-tuple-element.14.refs_1_), custom_call_target="tpu_custom_call" | custom-call | flops 1000 | tf_op jit(solution)/shard_map/reorder/pallas_call | solution.py:149
  12.3 0.4 %collective-permute-done.4.refs_0_ = bf16[192,512]{1,0:T(8,128)(2,1)S(1)} collective-permute-done((bf16[192,512]{1,0:T(8,128)(2,1)S(1)}, bf16[192,512]{1,0:T(8,128)(2,1)S(1)}, u32[]{:S(2)}, u32[]{:S(2)}) %collective-permute-start.4) | collective-permute-done | bytes 196640 | tf_op jit(solution)/shard_map/ppermute | solution.py:143
  12.7 2.1 %apply.1 = (f32[64,512]{1,0:T(8,128)S(1)}, s16[272,128]{1,0:T(8,128)(2,1)S(1)}, s16[272,128]{1,0:T(8,128)(2,1)S(1)}, s16[272,128]{1,0:T(8,128)(2,1)S(1)}) custom-call(s32[256]{0:T(256)S(1)} %get-tuple-element.12.meta_hbm, s32[16,1,256]{2,1,0:T(1,128)S(1)} %bitcast.7, bf16[16,8,16,256]{3,2,1,0:T(8,128)(2,1)S(1)} %copy-done, ...), custom_call_target="tpu_custom_call" | custom-call | tf_op jit(solution)/shard_map/apply/pallas_call | solution.py:177
  14.9 2.5 %collective-permute-start.5 = (s16[272,128]{1,0:T(8,128)(2,1)S(1)}, s16[272,128]{1,0:T(8,128)(2,1)S(1)}, u32[]{:S(2)}, u32[]{:S(2)}) collective-permute-start(s16[272,128]{1,0:T(8,128)(2,1)S(1)} %get-tuple-element.16), channel_id=1, source_target_pairs={{0,24},{8,16},{16,8},{24,0},{1,25},{9,17},{17,9},{25,1},{2,26},{10... | collective-permute-start | bytes 208904 | tf_op jit(solution)/shard_map/ppermute | solution.py:194
  17.4 0.5 %collective-permute-start.6 = (s16[272,128]{1,0:T(8,128)(2,1)S(1)}, s16[272,128]{1,0:T(8,128)(2,1)S(1)}, u32[]{:S(2)}, u32[]{:S(2)}) collective-permute-start(s16[272,128]{1,0:T(8,128)(2,1)S(1)} %get-tuple-element.17), channel_id=1, source_target_pairs={{0,16},{8,0},{16,24},{24,8},{1,17},{9,1},{17,25},{25,9},{2,18},{10... | collective-permute-start | bytes 208904 | tf_op jit(solution)/shard_map/ppermute | solution.py:194
  17.9 1.5 %collective-permute-start.7 = (s16[272,128]{1,0:T(8,128)(2,1)S(1)}, s16[272,128]{1,0:T(8,128)(2,1)S(1)}, u32[]{:S(2)}, u32[]{:S(2)}) collective-permute-start(s16[272,128]{1,0:T(8,128)(2,1)S(1)} %get-tuple-element.18), channel_id=1, source_target_pairs={{0,8},{8,24},{16,0},{24,16},{1,9},{9,25},{17,1},{25,17},{2,10},{10... | collective-permute-start | bytes 208904 | tf_op jit(solution)/shard_map/ppermute | solution.py:194
  19.4 0.9 %collective-permute-done.5.refs_0_ = s16[272,128]{1,0:T(8,128)(2,1)S(1)} collective-permute-done((s16[272,128]{1,0:T(8,128)(2,1)S(1)}, s16[272,128]{1,0:T(8,128)(2,1)S(1)}, u32[]{:S(2)}, u32[]{:S(2)}) %collective-permute-start.5) | collective-permute-done | bytes 69664 | tf_op jit(solution)/shard_map/ppermute | solution.py:194
  20.3 1.4 %collective-permute-done.6.refs_1_ = s16[272,128]{1,0:T(8,128)(2,1)S(1)} collective-permute-done((s16[272,128]{1,0:T(8,128)(2,1)S(1)}, s16[272,128]{1,0:T(8,128)(2,1)S(1)}, u32[]{:S(2)}, u32[]{:S(2)}) %collective-permute-start.6) | collective-permute-done | bytes 69664 | tf_op jit(solution)/shard_map/ppermute | solution.py:194
  21.7 0.5 %collective-permute-done.7.refs_2_ = s16[272,128]{1,0:T(8,128)(2,1)S(1)} collective-permute-done((s16[272,128]{1,0:T(8,128)(2,1)S(1)}, s16[272,128]{1,0:T(8,128)(2,1)S(1)}, u32[]{:S(2)}, u32[]{:S(2)}) %collective-permute-start.7) | collective-permute-done | bytes 69664 | tf_op jit(solution)/shard_map/ppermute | solution.py:194
  22.2 0.7 %finish.1 = f32[64,512]{1,0:T(8,128)} custom-call(f32[64,512]{1,0:T(8,128)S(1)} %get-tuple-element.15.own_ref, s16[272,128]{1,0:T(8,128)(2,1)S(1)} %collective-permute-done.5.refs_0_, s16[272,128]{1,0:T(8,128)(2,1)S(1)} %collective-permute-done.6.refs_1_, s16[272,128]{1,0:T(8,128)(2,1)S(1)} %collective-permute-done.7.refs_2_), custom_call_target="tpu_custom_call" | custom-call | tf_op jit(solution)/shard_map/finish/pallas_call | solution.py:195
  (12 shorter events, 0.0 us)
Async XLA Ops:
  0.0 10.8 %collective-permute-start.1 = (bf16[64,512]{1,0:T(8,128)(2,1)}, bf16[64,512]{1,0:T(8,128)(2,1)S(1)}, u32[]{:S(2)}, u32[]{:S(2)}) collective-permute-start(bf16[64,512]{1,0:T(8,128)(2,1)} %refs_0_.1), channel_id=1, source_target_pairs={{0,6},{1,7},{2,4},{3,5},{4,2},{5,3},{6,0},{7,1},{8,14},{9,15},{10,... | collective-permute-start | bytes 196616 | tf_op jit(solution)/shard_map/ppermute | solution.py:143
  5.0 2.0 %collective-permute-start = (bf16[64,512]{1,0:T(8,128)(2,1)}, bf16[64,512]{1,0:T(8,128)(2,1)S(1)}, u32[]{:S(2)}, u32[]{:S(2)}) collective-permute-start(bf16[64,512]{1,0:T(8,128)(2,1)} %refs_0_.1), channel_id=1, source_target_pairs={{0,1},{1,0},{2,3},{3,2},{4,5},{5,4},{6,7},{7,6},{8,9},{9,8},{10,11... | collective-permute-start | bytes 196616 | tf_op jit(solution)/shard_map/ppermute | solution.py:143
  5.1 6.1 %collective-permute-start.3 = (bf16[64,512]{1,0:T(8,128)(2,1)}, bf16[64,512]{1,0:T(8,128)(2,1)S(1)}, u32[]{:S(2)}, u32[]{:S(2)}) collective-permute-start(bf16[64,512]{1,0:T(8,128)(2,1)} %refs_0_.1), channel_id=1, source_target_pairs={{0,4},{1,5},{2,6},{3,7},{4,0},{5,1},{6,2},{7,3},{8,12},{9,13},{10,... | collective-permute-start | bytes 196616 | tf_op jit(solution)/shard_map/ppermute | solution.py:143
  5.1 6.1 %collective-permute-start.2 = (bf16[64,512]{1,0:T(8,128)(2,1)}, bf16[64,512]{1,0:T(8,128)(2,1)S(1)}, u32[]{:S(2)}, u32[]{:S(2)}) collective-permute-start(bf16[64,512]{1,0:T(8,128)(2,1)} %refs_0_.1), channel_id=1, source_target_pairs={{0,2},{1,3},{2,0},{3,1},{4,6},{5,7},{6,4},{7,5},{8,10},{9,11},{10,... | collective-permute-start | bytes 196616 | tf_op jit(solution)/shard_map/ppermute | solution.py:143
  6.4 0.7 %copy-start.4 = (s32[16,8]{0,1:T(8,128)S(1)}, s32[16,8]{0,1:T(8,128)}, u32[]{:S(2)}) copy-start(s32[16,8]{0,1:T(8,128)} %param.12) | copy-start | bytes 1540
  7.1 0.7 %copy-start.5 = (s32[1,1,2,8]{3,2,1,0:T(2,128)S(1)}, s32[1,1,2,8]{3,2,1,0:T(2,128)}, u32[]{:S(2)}) copy-start(s32[1,1,2,8]{3,2,1,0:T(2,128)} %param.14) | copy-start | bytes 196
  7.8 0.8 %copy-start.3 = (bf16[64,512]{1,0:T(8,128)(2,1)S(1)}, bf16[64,512]{1,0:T(8,128)(2,1)}, u32[]{:S(2)}) copy-start(bf16[64,512]{1,0:T(8,128)(2,1)} %refs_0_.1) | copy-start | bytes 196612
  8.6 4.1 %copy-start.1 = (bf16[16,8,16,256]{3,2,1,0:T(8,128)(2,1)S(1)}, bf16[16,8,16,256]{3,2,1,0:T(8,128)(2,1)}, u32[]{:S(2)}) copy-start(bf16[16,8,16,256]{3,2,1,0:T(8,128)(2,1)} %right_ref.1) | copy-start | bytes 3145732
  8.6 4.1 %copy-start.2 = (bf16[1,1,8,256,256]{4,3,2,1,0:T(8,128)(2,1)S(1)}, bf16[1,1,8,256,256]{4,3,2,1,0:T(8,128)(2,1)}, u32[]{:S(2)}) copy-start(bf16[1,1,8,256,256]{4,3,2,1,0:T(8,128)(2,1)} %param.13) | copy-start | bytes 3145732
  10.8 1.9 %copy-start = (bf16[16,8,16,256]{3,2,1,0:T(8,128)(2,1)S(1)}, bf16[16,8,16,256]{3,2,1,0:T(8,128)(2,1)}, u32[]{:S(2)}) copy-start(bf16[16,8,16,256]{3,2,1,0:T(8,128)(2,1)} %left_ref.1) | copy-start | bytes 3145732
  11.2 1.5 %collective-permute-start.4 = (bf16[192,512]{1,0:T(8,128)(2,1)S(1)}, bf16[192,512]{1,0:T(8,128)(2,1)S(1)}, u32[]{:S(2)}, u32[]{:S(2)}) collective-permute-start(bf16[192,512]{1,0:T(8,128)(2,1)S(1)} %constant_dynamic-update-slice_fusion.refs_0_), channel_id=1, source_target_pairs={{0,1},{1,0},{2,3},{3,2},{4,5},{5,4},{6,7},{7,6},{8,9},{9,8},{10,11... | collective-permute-start | bytes 589832 | tf_op jit(solution)/shard_map/ppermute | solution.py:143
  14.9 5.4 %collective-permute-start.5 = (s16[272,128]{1,0:T(8,128)(2,1)S(1)}, s16[272,128]{1,0:T(8,128)(2,1)S(1)}, u32[]{:S(2)}, u32[]{:S(2)}) collective-permute-start(s16[272,128]{1,0:T(8,128)(2,1)S(1)} %get-tuple-element.16), channel_id=1, source_target_pairs={{0,24},{8,16},{16,8},{24,0},{1,25},{9,17},{17,9},{25,1},{2,26},{10... | collective-permute-start | bytes 208904 | tf_op jit(solution)/shard_map/ppermute | solution.py:194
  17.4 4.3 %collective-permute-start.6 = (s16[272,128]{1,0:T(8,128)(2,1)S(1)}, s16[272,128]{1,0:T(8,128)(2,1)S(1)}, u32[]{:S(2)}, u32[]{:S(2)}) collective-permute-start(s16[272,128]{1,0:T(8,128)(2,1)S(1)} %get-tuple-element.17), channel_id=1, source_target_pairs={{0,16},{8,0},{16,24},{24,8},{1,17},{9,1},{17,25},{25,9},{2,18},{10... | collective-permute-start | bytes 208904 | tf_op jit(solution)/shard_map/ppermute | solution.py:194
  17.9 4.3 %collective-permute-start.7 = (s16[272,128]{1,0:T(8,128)(2,1)S(1)}, s16[272,128]{1,0:T(8,128)(2,1)S(1)}, u32[]{:S(2)}, u32[]{:S(2)}) collective-permute-start(s16[272,128]{1,0:T(8,128)(2,1)S(1)} %get-tuple-element.18), channel_id=1, source_target_pairs={{0,8},{8,24},{16,0},{24,16},{1,9},{9,25},{17,1},{25,17},{2,10},{10... | collective-permute-start | bytes 208904 | tf_op jit(solution)/shard_map/ppermute | solution.py:194

commit v7 on v5

--- a/solution.py
+++ b/solution.py
@@ -118,15 +118,21 @@
 
 
 def finish_kernel(own_ref, *refs):
-    *got_refs, out_ref = refs
+    *got_refs, out_ref, sum_ref, sems = refs
     rows = own_ref.shape[0]
     parts = own_ref.shape[1] // 128
     steps = [jnp.exp2(got_ref[parts * rows :].astype(F32)[:1]) for got_ref in got_refs]
+    copies = []
     for part in range(parts):
         total = own_ref[:, part * 128 : (part + 1) * 128]
         for got_ref, step in zip(got_refs, steps):
             total = total + got_ref[part * rows : (part + 1) * rows].astype(F32) * step
-        out_ref[:, part * 128 : (part + 1) * 128] = total
+        columns = slice(part * 128, (part + 1) * 128)
+        sum_ref[:, columns] = total
+        copies.append(pltpu.make_async_copy(sum_ref.at[:, columns], out_ref.at[:, columns], sems.at[part]))
+        copies[-1].start()
+    for copy in copies:
+        copy.wait()
 
 
 def local(sizes, adjoint, panel_order, left, right, tile_ranks, near_blocks, near_index, near_count):
@@ -188,7 +194,8 @@
         finish_kernel,
         out_shape=jax.ShapeDtypeStruct((rows, out_cols), F32),
         in_specs=[VMEM] * n_row,
-        out_specs=VMEM,
+        out_specs=ANY,
+        scratch_shapes=[pltpu.VMEM((rows, out_cols), F32), pltpu.SemaphoreType.DMA((out_cols // 128,))],
         compiler_params=pltpu.CompilerParams(vmem_limit_bytes=4 << 20),
         name="finish",
     )(out, *got)

time: 23.2 us -> 23.2 us (level)
  no operation moved by 1% of the time
where the time goes in v7:
time: 23.2 us; the launch traced here: 22.9 us
  starting transfers between devices  9.31 us (40%)
  Pallas kernels  6.06 us (26%)
  waiting for transfers between devices  4.5 us (19%)
  local copies, waits for them, and re-layouts  1.54 us (7%)
  between operations  0.77 us (3%)
  other arithmetic  0.73 us (3%)
    ppermute x8, starting transfers between devices, local(): lax.ppermute(x, axis, [(i, i ^ d) for i in range(n)])  9.31 us
    ppermute x8, waiting for transfers between devices, local(): lax.ppermute(x, axis, [(i, i ^ d) for i in range(n)])  4.5 us
    pallas_call x2, Pallas kernels, reorder(): pl.pallas_call(functools.partial(reorder_kernel, distances, part is None)...  3.21 us
    pallas_call x1, Pallas kernels, local(): pl.pallas_call(functools.partial(main_kernel, last_off), out_shape=[jax.S...  2.14 us
    unnamed x12, local copies, waits for them, and re-layouts  1.52 us
    xor x1, other arithmetic, local(): jnp.bitwise_xor(panel_order, lax.axis_index('col') * own_cols)  0.73 us
    pallas_call x1, Pallas kernels, local(): pl.pallas_call(finish_kernel, out_shape=jax.ShapeDtypeStruct((rows, out_c...  0.71 us
  transfers between devices with their start and end apart: 8, of which 5 were waited for; matrix products, arithmetic and copies ran while one was open for 3% of the time, Pallas kernels for 14%

profile of v7, /device:TPU:0, one launch (start us, length us, event | category | flops | bytes accessed | tf_op | source)
XLA Modules:
  0.0 22.9 jit_solution(2120756969889757697)
XLA Ops:
  0.0 5.0 %collective-permute-start.1 = (bf16[64,512]{1,0:T(8,128)(2,1)}, bf16[64,512]{1,0:T(8,128)(2,1)S(1)}, u32[]{:S(2)}, u32[]{:S(2)}) collective-permute-start(bf16[64,512]{1,0:T(8,128)(2,1)} %refs_0_.1), channel_id=1, source_target_pairs={{0,6},{1,7},{2,4},{3,5},{4,2},{5,3},{6,0},{7,1},{8,14},{9,15},{10,... | collective-permute-start | bytes 196616 | tf_op jit(solution)/shard_map/ppermute | solution.py:142
  5.1 0.0 collective-permute-start.3
  5.1 0.6 %collective-permute-start.2 = (bf16[64,512]{1,0:T(8,128)(2,1)}, bf16[64,512]{1,0:T(8,128)(2,1)S(1)}, u32[]{:S(2)}, u32[]{:S(2)}) collective-permute-start(bf16[64,512]{1,0:T(8,128)(2,1)} %refs_0_.1), channel_id=1, source_target_pairs={{0,2},{1,3},{2,0},{3,1},{4,6},{5,7},{6,4},{7,5},{8,10},{9,11},{10,... | collective-permute-start | bytes 196616 | tf_op jit(solution)/shard_map/ppermute | solution.py:142
  5.7 0.7 %broadcast_xor_fusion = s32[1,4096]{1,0:T(1,128)S(1)} fusion(s32[1,4096]{1,0:T(1,128)} %param.9, s32[]{:T(128)S(6)} %mul.3), kind=kLoop, calls=%fused_computation | loop fusion | flops 4096 | bytes 32772 | tf_op jit(solution)/shard_map/xor | solution.py:161
  6.4 0.0 copy-start.4
  7.1 0.0 copy-start.5
  7.1 0.7 %copy-done.5 = s32[1,1,2,8]{3,2,1,0:T(2,128)S(1)} copy-done((s32[1,1,2,8]{3,2,1,0:T(2,128)S(1)}, s32[1,1,2,8]{3,2,1,0:T(2,128)}, u32[]{:S(2)}) %copy-start.5) | copy-done | bytes 88
  7.8 0.8 %copy-done.3 = bf16[64,512]{1,0:T(8,128)(2,1)S(1)} copy-done((bf16[64,512]{1,0:T(8,128)(2,1)S(1)}, bf16[64,512]{1,0:T(8,128)(2,1)}, u32[]{:S(2)}) %copy-start.3) | copy-done | bytes 65560
  8.6 2.2 %reorder.2 = (bf16[16,64,256]{2,1,0:T(8,128)(2,1)S(1)}, bf16[192,512]{1,0:T(8,128)(2,1)S(1)}, s32[256]{0:T(256)S(1)}) custom-call(s32[16,1,256]{2,1,0:T(1,128)S(1)} %bitcast.5, bf16[64,512]{1,0:T(8,128)(2,1)S(1)} %copy-done.3, bf16[64,512]{1,0:T(8,128)(2,1)S(1)} %collective-permute-done.refs_1_, s32[1,1]{1,0:T(1,128)S(6)} %copy.12.refs_2_, ...), custom_call_target="tpu_custom_call" | custom-call | flops 536870912 | tf_op jit(solution)/shard_map/reorder/pallas_call | solution.py:148
  10.8 0.0 copy-start
  10.8 0.0 collective-permute-done.1
  10.8 0.3 %collective-permute-done.2 = bf16[64,512]{1,0:T(8,128)(2,1)S(1)} collective-permute-done((bf16[64,512]{1,0:T(8,128)(2,1)}, bf16[64,512]{1,0:T(8,128)(2,1)S(1)}, u32[]{:S(2)}, u32[]{:S(2)}) %collective-permute-start.2) | collective-permute-done | bytes 65568 | tf_op jit(solution)/shard_map/ppermute | solution.py:142
  11.2 0.0 collective-permute-done.3
  11.2 0.1 collective-permute-start.4
  11.3 1.0 %reorder.3.part_ref = bf16[16,64,256]{2,1,0:T(8,128)(2,1)S(1)} custom-call(s32[16,1,256]{2,1,0:T(1,128)S(1)} %bitcast.6, bf16[192,512]{1,0:T(8,128)(2,1)S(1)} %constant_dynamic-update-slice_fusion.refs_0_, bf16[16,64,256]{2,1,0:T(8,128)(2,1)S(1)} %get-tuple-element.14.refs_1_), custom_call_target="tpu_custom_call" | custom-call | flops 1000 | tf_op jit(solution)/shard_map/reorder/pallas_call | solution.py:148
  12.3 0.4 %collective-permute-done.4.refs_0_ = bf16[192,512]{1,0:T(8,128)(2,1)S(1)} collective-permute-done((bf16[192,512]{1,0:T(8,128)(2,1)S(1)}, bf16[192,512]{1,0:T(8,128)(2,1)S(1)}, u32[]{:S(2)}, u32[]{:S(2)}) %collective-permute-start.4) | collective-permute-done | bytes 196640 | tf_op jit(solution)/shard_map/ppermute | solution.py:142
  12.7 2.1 %apply.1 = (f32[64,512]{1,0:T(8,128)S(1)}, s16[272,128]{1,0:T(8,128)(2,1)S(1)}, s16[272,128]{1,0:T(8,128)(2,1)S(1)}, s16[272,128]{1,0:T(8,128)(2,1)S(1)}) custom-call(s32[256]{0:T(256)S(1)} %get-tuple-element.12.meta_hbm, s32[16,1,256]{2,1,0:T(1,128)S(1)} %bitcast.7, bf16[16,8,16,256]{3,2,1,0:T(8,128)(2,1)S(1)} %copy-done, ...), custom_call_target="tpu_custom_call" | custom-call | tf_op jit(solution)/shard_map/apply/pallas_call | solution.py:176
  14.9 2.5 %collective-permute-start.5 = (s16[272,128]{1,0:T(8,128)(2,1)S(1)}, s16[272,128]{1,0:T(8,128)(2,1)S(1)}, u32[]{:S(2)}, u32[]{:S(2)}) collective-permute-start(s16[272,128]{1,0:T(8,128)(2,1)S(1)} %get-tuple-element.16), channel_id=1, source_target_pairs={{0,24},{8,16},{16,8},{24,0},{1,25},{9,17},{17,9},{25,1},{2,26},{10... | collective-permute-start | bytes 208904 | tf_op jit(solution)/shard_map/ppermute | solution.py:142
  17.4 0.5 %collective-permute-start.6 = (s16[272,128]{1,0:T(8,128)(2,1)S(1)}, s16[272,128]{1,0:T(8,128)(2,1)S(1)}, u32[]{:S(2)}, u32[]{:S(2)}) collective-permute-start(s16[272,128]{1,0:T(8,128)(2,1)S(1)} %get-tuple-element.17), channel_id=1, source_target_pairs={{0,16},{8,24},{16,0},{24,8},{1,17},{9,25},{17,1},{25,9},{2,18},{10... | collective-permute-start | bytes 208904 | tf_op jit(solution)/shard_map/ppermute | solution.py:142
  17.9 0.5 %collective-permute-start.7 = (s16[272,128]{1,0:T(8,128)(2,1)S(1)}, s16[272,128]{1,0:T(8,128)(2,1)S(1)}, u32[]{:S(2)}, u32[]{:S(2)}) collective-permute-start(s16[272,128]{1,0:T(8,128)(2,1)S(1)} %get-tuple-element.18), channel_id=1, source_target_pairs={{0,8},{8,0},{16,24},{24,16},{1,9},{9,1},{17,25},{25,17},{2,10},{10... | collective-permute-start | bytes 208904 | tf_op jit(solution)/shard_map/ppermute | solution.py:142
  18.4 1.7 %collective-permute-done.5.refs_0_ = s16[272,128]{1,0:T(8,128)(2,1)S(1)} collective-permute-done((s16[272,128]{1,0:T(8,128)(2,1)S(1)}, s16[272,128]{1,0:T(8,128)(2,1)S(1)}, u32[]{:S(2)}, u32[]{:S(2)}) %collective-permute-start.5) | collective-permute-done | bytes 69664 | tf_op jit(solution)/shard_map/ppermute | solution.py:142
  20.2 1.5 %collective-permute-done.6.refs_1_ = s16[272,128]{1,0:T(8,128)(2,1)S(1)} collective-permute-done((s16[272,128]{1,0:T(8,128)(2,1)S(1)}, s16[272,128]{1,0:T(8,128)(2,1)S(1)}, u32[]{:S(2)}, u32[]{:S(2)}) %collective-permute-start.6) | collective-permute-done | bytes 69664 | tf_op jit(solution)/shard_map/ppermute | solution.py:142
  21.7 0.5 %collective-permute-done.7.refs_2_ = s16[272,128]{1,0:T(8,128)(2,1)S(1)} collective-permute-done((s16[272,128]{1,0:T(8,128)(2,1)S(1)}, s16[272,128]{1,0:T(8,128)(2,1)S(1)}, u32[]{:S(2)}, u32[]{:S(2)}) %collective-permute-start.7) | collective-permute-done | bytes 69664 | tf_op jit(solution)/shard_map/ppermute | solution.py:142
  22.2 0.7 %finish.1 = f32[64,512]{1,0:T(8,128)} custom-call(f32[64,512]{1,0:T(8,128)S(1)} %get-tuple-element.15.own_ref, s16[272,128]{1,0:T(8,128)(2,1)S(1)} %collective-permute-done.5.refs_0_, s16[272,128]{1,0:T(8,128)(2,1)S(1)} %collective-permute-done.6.refs_1_, s16[272,128]{1,0:T(8,128)(2,1)S(1)} %collective-permute-done.7.refs_2_), custom_call_target="tpu_custom_call" | custom-call | tf_op jit(solution)/shard_map/finish/pallas_call | solution.py:193
  (12 shorter events, 0.0 us)
Async XLA Ops:
  0.0 10.8 %collective-permute-start.1 = (bf16[64,512]{1,0:T(8,128)(2,1)}, bf16[64,512]{1,0:T(8,128)(2,1)S(1)}, u32[]{:S(2)}, u32[]{:S(2)}) collective-permute-start(bf16[64,512]{1,0:T(8,128)(2,1)} %refs_0_.1), channel_id=1, source_target_pairs={{0,6},{1,7},{2,4},{3,5},{4,2},{5,3},{6,0},{7,1},{8,14},{9,15},{10,... | collective-permute-start | bytes 196616 | tf_op jit(solution)/shard_map/ppermute | solution.py:142
  5.0 2.0 %collective-permute-start = (bf16[64,512]{1,0:T(8,128)(2,1)}, bf16[64,512]{1,0:T(8,128)(2,1)S(1)}, u32[]{:S(2)}, u32[]{:S(2)}) collective-permute-start(bf16[64,512]{1,0:T(8,128)(2,1)} %refs_0_.1), channel_id=1, source_target_pairs={{0,1},{1,0},{2,3},{3,2},{4,5},{5,4},{6,7},{7,6},{8,9},{9,8},{10,11... | collective-permute-start | bytes 196616 | tf_op jit(solution)/shard_map/ppermute | solution.py:142
  5.1 6.1 %collective-permute-start.3 = (bf16[64,512]{1,0:T(8,128)(2,1)}, bf16[64,512]{1,0:T(8,128)(2,1)S(1)}, u32[]{:S(2)}, u32[]{:S(2)}) collective-permute-start(bf16[64,512]{1,0:T(8,128)(2,1)} %refs_0_.1), channel_id=1, source_target_pairs={{0,4},{1,5},{2,6},{3,7},{4,0},{5,1},{6,2},{7,3},{8,12},{9,13},{10,... | collective-permute-start | bytes 196616 | tf_op jit(solution)/shard_map/ppermute | solution.py:142
  5.1 6.1 %collective-permute-start.2 = (bf16[64,512]{1,0:T(8,128)(2,1)}, bf16[64,512]{1,0:T(8,128)(2,1)S(1)}, u32[]{:S(2)}, u32[]{:S(2)}) collective-permute-start(bf16[64,512]{1,0:T(8,128)(2,1)} %refs_0_.1), channel_id=1, source_target_pairs={{0,2},{1,3},{2,0},{3,1},{4,6},{5,7},{6,4},{7,5},{8,10},{9,11},{10,... | collective-permute-start | bytes 196616 | tf_op jit(solution)/shard_map/ppermute | solution.py:142
  6.4 0.7 %copy-start.4 = (s32[16,8]{0,1:T(8,128)S(1)}, s32[16,8]{0,1:T(8,128)}, u32[]{:S(2)}) copy-start(s32[16,8]{0,1:T(8,128)} %param.12) | copy-start | bytes 1540
  7.1 0.7 %copy-start.5 = (s32[1,1,2,8]{3,2,1,0:T(2,128)S(1)}, s32[1,1,2,8]{3,2,1,0:T(2,128)}, u32[]{:S(2)}) copy-start(s32[1,1,2,8]{3,2,1,0:T(2,128)} %param.14) | copy-start | bytes 196
  7.8 0.8 %copy-start.3 = (bf16[64,512]{1,0:T(8,128)(2,1)S(1)}, bf16[64,512]{1,0:T(8,128)(2,1)}, u32[]{:S(2)}) copy-start(bf16[64,512]{1,0:T(8,128)(2,1)} %refs_0_.1) | copy-start | bytes 196612
  8.6 4.1 %copy-start.1 = (bf16[16,8,16,256]{3,2,1,0:T(8,128)(2,1)S(1)}, bf16[16,8,16,256]{3,2,1,0:T(8,128)(2,1)}, u32[]{:S(2)}) copy-start(bf16[16,8,16,256]{3,2,1,0:T(8,128)(2,1)} %right_ref.1) | copy-start | bytes 3145732
  8.6 4.1 %copy-start.2 = (bf16[1,1,8,256,256]{4,3,2,1,0:T(8,128)(2,1)S(1)}, bf16[1,1,8,256,256]{4,3,2,1,0:T(8,128)(2,1)}, u32[]{:S(2)}) copy-start(bf16[1,1,8,256,256]{4,3,2,1,0:T(8,128)(2,1)} %param.13) | copy-start | bytes 3145732
  10.8 1.9 %copy-start = (bf16[16,8,16,256]{3,2,1,0:T(8,128)(2,1)S(1)}, bf16[16,8,16,256]{3,2,1,0:T(8,128)(2,1)}, u32[]{:S(2)}) copy-start(bf16[16,8,16,256]{3,2,1,0:T(8,128)(2,1)} %left_ref.1) | copy-start | bytes 3145732
  11.2 1.5 %collective-permute-start.4 = (bf16[192,512]{1,0:T(8,128)(2,1)S(1)}, bf16[192,512]{1,0:T(8,128)(2,1)S(1)}, u32[]{:S(2)}, u32[]{:S(2)}) collective-permute-start(bf16[192,512]{1,0:T(8,128)(2,1)S(1)} %constant_dynamic-update-slice_fusion.refs_0_), channel_id=1, source_target_pairs={{0,1},{1,0},{2,3},{3,2},{4,5},{5,4},{6,7},{7,6},{8,9},{9,8},{10,11... | collective-permute-start | bytes 589832 | tf_op jit(solution)/shard_map/ppermute | solution.py:142
  14.9 5.3 %collective-permute-start.5 = (s16[272,128]{1,0:T(8,128)(2,1)S(1)}, s16[272,128]{1,0:T(8,128)(2,1)S(1)}, u32[]{:S(2)}, u32[]{:S(2)}) collective-permute-start(s16[272,128]{1,0:T(8,128)(2,1)S(1)} %get-tuple-element.16), channel_id=1, source_target_pairs={{0,24},{8,16},{16,8},{24,0},{1,25},{9,17},{17,9},{25,1},{2,26},{10... | collective-permute-start | bytes 208904 | tf_op jit(solution)/shard_map/ppermute | solution.py:142
  17.4 4.3 %collective-permute-start.6 = (s16[272,128]{1,0:T(8,128)(2,1)S(1)}, s16[272,128]{1,0:T(8,128)(2,1)S(1)}, u32[]{:S(2)}, u32[]{:S(2)}) collective-permute-start(s16[272,128]{1,0:T(8,128)(2,1)S(1)} %get-tuple-element.17), channel_id=1, source_target_pairs={{0,16},{8,24},{16,0},{24,8},{1,17},{9,25},{17,1},{25,9},{2,18},{10... | collective-permute-start | bytes 208904 | tf_op jit(solution)/shard_map/ppermute | solution.py:142
  17.9 4.3 %collective-permute-start.7 = (s16[272,128]{1,0:T(8,128)(2,1)S(1)}, s16[272,128]{1,0:T(8,128)(2,1)S(1)}, u32[]{:S(2)}, u32[]{:S(2)}) collective-permute-start(s16[272,128]{1,0:T(8,128)(2,1)S(1)} %get-tuple-element.18), channel_id=1, source_target_pairs={{0,8},{8,0},{16,24},{24,16},{1,9},{9,1},{17,25},{25,17},{2,10},{10... | collective-permute-start | bytes 208904 | tf_op jit(solution)/shard_map/ppermute | solution.py:142
